TPU v7x, 128 devices: a whole 4x4x4 slice. The times are simulated.
128 devices in a mesh: rep: 64 (over y, x, z_hi, core), shard: 2 (over z_lo).
Axes of the slice: x: 4, y: 4, z: 4 (z_hi: 2, z_lo: 2; z = z_hi * 2 + z_lo), core: 2. Of those that a mesh axis runs over, the one named last changes fastest.
Arguments:
- tokens: bfloat16 [24576, 768], P(('rep', 'shard')), may hold values from -6 to 6
- cotangent: bfloat16 [24576, 768], P(('rep', 'shard')), may hold values from -6 to 6
- attn_gain: bfloat16 [768], P('shard'), may hold values from 0.5 to 1.5
- w_qkv: bfloat16 [768, 2304], P('shard'), may hold values from -0.21875 to 0.21875
- w_out: bfloat16 [768, 768], P('shard'), may hold values from -1.75 to 1.75
- rel_bias: bfloat16 [32, 12], P('shard'), may hold values from -3 to 3
- buckets: int32 [384], replicated, may hold values from 0 to 31, as said below
- ffn_gain: bfloat16 [768], P('shard'), may hold values from 0.5 to 1.5
- w_router: bfloat16 [768, 64], P('shard'), may hold values from -0.21875 to 0.21875
- w_in: bfloat16 [64, 768, 3072], P('rep', None, 'shard'), may hold values from -0.21875 to 0.21875
- w_back: bfloat16 [64, 3072, 768], P('rep', 'shard'), may hold values from -6 to 6
- choice_ids: int32 [24576, 2], P(('rep', 'shard')), may hold values from 0 to 63, all different within a row; in each aligned block of 192 rows (0 to 191, 192 to 383, ...) at most 7 rows name the same one
Outputs:
- layer_out: bfloat16 [24576, 768], P(('rep', 'shard'))
- grad_tokens: float32 [24576, 768], P(('rep', 'shard'))
- grad_attn_gain: float32 [768], P('shard')
- grad_w_qkv: float32 [768, 2304], P('shard')
- grad_w_out: float32 [768, 768], P('shard')
- grad_rel_bias: float32 [32, 12], P('shard')
- grad_ffn_gain: float32 [768], P('shard')
- grad_w_router: float32 [768, 64], P('shard')
- grad_w_in: float32 [64, 768, 3072], P('rep', None, 'shard')
- grad_w_back: float32 [64, 3072, 768], P('rep', 'shard')
Inputs may be any that keep to these rules, and one draw needn't show every extreme that they name: buckets[0] is 0; from one distance to the next the entry stays or rises by one, and it reaches 31. `choice_ids`: the two experts of a row differ; among the rows of one device no expert is named more than 7 times, and in every draw some expert is named exactly 7 times by the rows of some device.
All inputs are finite; a program needn't handle non-finite values.
Results may differ from a plain program's by a relative error of at most 0.018.
Values may be sent and summed in bfloat16 or wider, within the bound.
A program may use at most 128 MiB of HBM per device.

v0:
```python
import functools

import jax
import jax.numpy as jnp
from jax import lax
from jax.experimental import pallas as pl
from jax.experimental.pallas import tpu as pltpu
from jax.sharding import PartitionSpec as P

EPSILON = 1e-06
MASKED = -1e30
MESH = pl.DeviceIdType.MESH
VMEM_SPEC = pl.BlockSpec(memory_space=pltpu.VMEM)
F32 = jnp.float32
BF16 = jnp.bfloat16


def greet_all(count):
    me = 2 * lax.axis_index("rep") + lax.axis_index("shard")
    barrier = pltpu.get_barrier_semaphore()

    def signal(step, carry):
        to = lax.rem(me + step, count)
        pl.semaphore_signal(
            barrier, inc=1, device_id=(to // 2, lax.rem(to, 2)), device_id_type=MESH
        )
        return carry

    lax.fori_loop(1, count, signal, 0)
    pl.semaphore_wait(barrier, count - 1)


def send_blocks(source_of, target, count, send, recv):
    me = 2 * lax.axis_index("rep") + lax.axis_index("shard")

    def start(step, carry):
        to = lax.rem(me + step, count)
        pltpu.make_async_remote_copy(
            source_of(to),
            target.at[me],
            send,
            recv,
            (to // 2, lax.rem(to, 2)),
            device_id_type=MESH,
        ).start()
        return carry

    lax.fori_loop(1, count, start, 0)


def wait_blocks(target, count, send, recv):
    rep, mine = lax.axis_index("rep"), lax.axis_index("shard")
    most = target.at[pl.ds(0, count - 1)]
    pltpu.make_async_remote_copy(
        most, most, send, recv, (rep, 1 - mine), device_id_type=MESH
    ).wait()


def up(number, step):
    return -(-number // step) * step


def greet(peers):
    barrier = pltpu.get_barrier_semaphore()
    for peer in peers:
        pl.semaphore_signal(barrier, inc=1, device_id=peer, device_id_type=MESH)
    pl.semaphore_wait(barrier, len(peers))


def iota(shape, axis):
    return lax.broadcasted_iota(jnp.int32, shape, axis)


def dot(a, b, contract):
    return lax.dot_general(a, b, (contract, ((), ())), preferred_element_type=F32)


def matmul(a, b):
    return dot(a, b, ((1,), (0,)))


def matmul_t(a, b):
    return dot(a, b, ((1,), (1,)))


def t_matmul(a, b):
    return dot(a, b, ((0,), (0,)))


def two_parts(values):
    high = values.astype(BF16)
    return high, (values - high.astype(F32)).astype(BF16)


def rms_factor(values):
    return lax.rsqrt(jnp.mean(values * values, axis=-1, keepdims=True) + EPSILON)


def gain_row(small_ref, half, first):
    blocks = half // 128
    pieces = [
        small_ref[side, pl.ds(half + first + i, 1), :].astype(F32)
        for side in range(2)
        for i in range(blocks)
    ]
    return jnp.concatenate(pieces, axis=1)


def router_weight(small_ref, half):
    return jnp.concatenate([small_ref[0, :half, :], small_ref[1, :half, :]], axis=0)


def lifted(block, capacity):
    count = block.shape[0]
    shift = capacity.bit_length() - 1
    source, slot = iota((count, count), 1), iota((count, count), 0)
    carrier = (source == ((slot >> shift) << shift) + capacity - 1).astype(F32).astype(BF16)
    carried = matmul(carrier, block)
    lane, slot = iota((count, 128), 1), iota((count, 128), 0)
    mask = ((lane & (capacity - 1)) == (slot & (capacity - 1))) & (lane < 2 * capacity)
    return jnp.sum(jnp.where(mask, carried, 0.0), axis=1, keepdims=True)


def lowered(column, capacity):
    count = column.shape[0]
    shift = capacity.bit_length() - 1
    target, slot = iota((count, count), 0), iota((count, count), 1)
    carrier = (target == ((slot >> shift) << shift) + capacity - 1).astype(F32).astype(BF16)
    lane, slot = iota((count, 128), 1), iota((count, 128), 0) & (capacity - 1)
    high, low = two_parts(column)
    spread = jnp.where(lane == slot, high.astype(F32), 0.0)
    spread = spread + jnp.where(lane == slot + capacity, low.astype(F32), 0.0)
    return matmul(carrier, spread.astype(BF16))


def front_kernel(
    sizes,
    dims,
    tok_ref,
    small_ref,
    wqkv_ref,
    wout_ref,
    bucket_ref,
    dispatch_ref,
    gout_ref,
    n1_ref,
    proj_ref,
    chance_ref,
    mixed_ref,
    w_all,
    small_all,
    hidden_ref,
    n2_ref,
    router_ref,
    arrived_ref,
    grad_rows_ref,
    tok_all,
    bias_rows,
    part_out,
    part_in,
    outgoing,
    outgoing_grads,
    send,
    recv,
    local,
):
    heads, experts, capacity, buckets = dims
    ys, xs, zs = sizes
    rows, width = tok_ref.shape
    half = width // 2
    seq = 2 * rows
    own_heads = heads // 2
    head = width // heads
    slots = experts * capacity
    rep, mine = lax.axis_index("rep"), lax.axis_index("shard")
    other = 1 - mine
    core = lax.rem(rep, 2)
    peer = (rep, other)
    core_peer = (rep + 1 - 2 * core, mine)
    devices = 2 * experts
    me = 2 * rep + mine
    if zs == 2:
        z = lax.rem(rep // 2, 2)
        far_peer = (rep + 2 * (1 - 2 * z), other)
    greet_all(devices)

    def remote(i, source, target, to):
        copy = pltpu.make_async_remote_copy(
            source, target, send.at[i], recv.at[i], to, device_id_type=MESH
        )
        copy.start()
        return copy

    small_copy = remote(0, small_ref, small_all.at[mine], peer)
    near = half // 2 if zs == 1 else up(half // 12, 16)
    fetched = [(peer, 0, near)]
    if zs == 2:
        fetched.append((far_peer, near, half // 2 - near))
    weight_copies = []
    for j, (to, first, count) in enumerate(fetched):
        at = pl.ds(pl.multiple_of(core * (half // 2) + first, 16), count)
        for block in range(3):
            theirs = pl.ds(pl.multiple_of((2 * block + other) * half, 128), half)
            weight_copies.append(
                remote(
                    2 + 3 * j + block,
                    wqkv_ref.at[at, theirs],
                    w_all.at[mine, at, pl.ds(block * half, half)],
                    to,
                )
            )
    tok_copy = remote(1, tok_ref, tok_all.at[mine], peer)
    kept = [
        pltpu.make_async_copy(tok_ref, tok_all.at[mine], local.at[0]),
        pltpu.make_async_copy(small_ref, small_all.at[mine], local.at[1]),
    ]
    for block in range(3):
        ours = pl.ds(pl.multiple_of((2 * block + mine) * half, 128), half)
        kept.append(
            pltpu.make_async_copy(
                wqkv_ref.at[:, ours], w_all.at[mine, :, pl.ds(block * half, half)], local.at[2 + block]
            )
        )
    for copy in kept:
        copy.start()
    for copy in kept:
        copy.wait()
    small_copy.wait()

    table = jnp.concatenate([small_all[0, half + 16 :, :], small_all[1, half + 16 :, :]], axis=0)
    levels = iota((buckets, 2 * seq), 0)
    one_hot = (levels == bucket_ref[...]).astype(F32).astype(BF16)
    bias_rows[...] = t_matmul(table, one_hot)
    gain_one = gain_row(small_all, half, 0)
    gain_two = gain_row(small_all, half, half // 128)
    dispatch = dispatch_ref[...]
    blocks = t_matmul(dispatch, gout_ref[...]).reshape(experts, capacity, width)
    outgoing_grads[...] = blocks.astype(BF16)

    for copy in weight_copies:
        copy.wait()
    got = w_all.at[other, pl.ds(pl.multiple_of(core * (half // 2), 16), half // 2)]
    passed = remote(8, got, got, core_peer)
    send_blocks(
        lambda to: outgoing_grads.at[to // 2], grad_rows_ref, devices, send.at[10], recv.at[10]
    )
    own_block = pltpu.make_async_copy(outgoing_grads.at[rep], grad_rows_ref.at[me], local.at[0])
    own_block.start()
    tok_copy.wait()
    for side in range(2):
        values = tok_all[side].astype(F32)
        n1_ref[side * rows : (side + 1) * rows, :] = (
            values * rms_factor(values) * gain_one
        ).astype(BF16)
    passed.wait()
    normed = n1_ref[...]
    for block in range(3):
        columns = pl.ds(block * half, half)
        total = matmul(normed[:, :half], w_all[0, :, columns])
        total = total + matmul(normed[:, half:], w_all[1, :, columns])
        proj_ref[:, columns] = total.astype(BF16)

    scale = head ** (-0.5)
    causal = iota((seq, seq), 0) >= iota((seq, seq), 1)
    for h in range(own_heads):
        at = h * head
        query = proj_ref[:, at : at + head]
        key = proj_ref[:, half + at : half + at + head]
        value = proj_ref[:, 2 * half + at : 2 * half + at + head]
        row = bias_rows[pl.ds(mine * own_heads + h, 1), :]
        bias = pltpu.roll(
            jnp.broadcast_to(row, (seq, 2 * seq)), 0, 1, stride=1, stride_axis=0
        )[:, :seq]
        scores = jnp.where(causal, matmul_t(query, key) * scale + bias, MASKED)
        raised = jnp.exp(scores - jnp.max(scores, axis=-1, keepdims=True))
        chance = (raised / jnp.sum(raised, axis=-1, keepdims=True)).astype(BF16)
        chance_ref[h] = chance
        mixed_ref[:, at : at + head] = matmul(chance, value).astype(BF16)

    theirs = pl.ds(pl.multiple_of(other * rows, 16), rows)
    ours = pl.ds(pl.multiple_of(mine * rows, 16), rows)
    part_out[...] = matmul(mixed_ref[theirs, :], wout_ref[...]).astype(BF16)
    part_copy = remote(9, part_out, part_in, peer)
    hidden = tok_ref[...].astype(F32) + matmul(mixed_ref[ours, :], wout_ref[...])
    part_copy.wait()
    hidden = hidden + part_in[...].astype(F32)
    hidden_ref[...] = hidden
    normed = (hidden * rms_factor(hidden) * gain_two).astype(BF16)
    n2_ref[...] = normed
    logits = matmul(normed, router_weight(small_all, half))
    logits = jnp.where(iota((rows, 128), 1) < experts, logits, MASKED)
    raised = jnp.exp(logits - jnp.max(logits, axis=-1, keepdims=True))
    router = raised / jnp.sum(raised, axis=-1, keepdims=True)
    router_ref[...] = router

    shift = capacity.bit_length() - 1
    spread = (iota((128, slots), 0) == (iota((128, slots), 1) >> shift)).astype(F32).astype(BF16)
    row_of, slot_of = iota((slots, slots), 0), iota((slots, slots), 1)
    carrier = ((row_of & (capacity - 1)) == capacity - 1) & (
        (row_of >> shift) == (slot_of >> shift)
    )
    place = iota((slots, 128), 0) & (capacity - 1)
    gates = jnp.zeros((slots, 128), F32)
    for i, part in enumerate(two_parts(router)):
        gate = jnp.sum(matmul(part, spread) * dispatch.astype(F32), axis=0, keepdims=True)
        left = jnp.where(carrier, gate, 0.0).astype(BF16)
        right = (place == iota((slots, 128), 1) - i * capacity).astype(F32).astype(BF16)
        gates = gates + matmul(left, right)
    sent = t_matmul(dispatch, normed)
    first = (sent[:, :128] + gates).reshape(experts, capacity, 128)
    outgoing[...] = sent.reshape(experts, capacity, width).astype(BF16)
    outgoing[:, :, :128] = first.astype(BF16)
    send_blocks(lambda to: outgoing.at[to // 2], arrived_ref, devices, send.at[11], recv.at[11])
    own_block.wait()
    own_block = pltpu.make_async_copy(outgoing.at[rep], arrived_ref.at[me], local.at[0])
    own_block.start()
    own_block.wait()
    wait_blocks(grad_rows_ref, devices, send.at[10], recv.at[10])
    wait_blocks(arrived_ref, devices, send.at[11], recv.at[11])


def front(sizes, dims, tokens, small, w_qkv, w_out, bucket_row, dispatch, cotangent):
    rows, width = tokens.shape
    heads, experts, capacity, buckets = dims
    half, seq, slots = width // 2, 2 * rows, experts * capacity
    shapes = [
        ((seq, width), BF16),
        ((seq, 3 * half), BF16),
        ((heads // 2, seq, seq), BF16),
        ((seq, half), BF16),
        ((2, half, 3 * half), BF16),
        ((2,) + small.shape, BF16),
        ((rows, width), F32),
        ((rows, width), BF16),
        ((rows, 128), F32),
        ((2 * experts, capacity, width), BF16),
        ((2 * experts, capacity, width), BF16),
    ]
    return pl.pallas_call(
        functools.partial(front_kernel, sizes, dims),
        out_shape=[jax.ShapeDtypeStruct(*shape) for shape in shapes],
        in_specs=[VMEM_SPEC] * 7,
        out_specs=[VMEM_SPEC] * len(shapes),
        scratch_shapes=[
            pltpu.VMEM((2, rows, width), BF16),
            pltpu.VMEM((128, 2 * seq), F32),
            pltpu.VMEM((rows, width), BF16),
            pltpu.VMEM((rows, width), BF16),
            pltpu.VMEM((experts, capacity, width), BF16),
            pltpu.VMEM((experts, capacity, width), BF16),
            pltpu.SemaphoreType.DMA((12,)),
            pltpu.SemaphoreType.DMA((12,)),
            pltpu.SemaphoreType.DMA((5,)),
        ],
        compiler_params=pltpu.CompilerParams(
            collective_id=0, has_side_effects=True, vmem_limit_bytes=48 * 2**20
        ),
        cost_estimate=pl.CostEstimate(flops=30 * 10**9, bytes_accessed=10**8, transcendentals=10**6),
    )(tokens, small, w_qkv, w_out, bucket_row, dispatch, cotangent)


def expert_kernel(
    capacity,
    rows_ref,
    grads_ref,
    in_ref,
    back_ref,
    active_ref,
    d_pre_ref,
    sent_ref,
    result_ref,
    d_result_ref,
):
    rows = rows_ref[...]
    grads = grads_ref[...]
    gate = lifted(rows[:, :128], capacity)
    d_result_ref[...] = (gate * grads.astype(F32)).astype(BF16)
    hidden = in_ref.shape[1]
    step = min(hidden, 512)
    root = 0.7978845608028654
    sent, result, d_gate = 0.0, 0.0, 0.0
    for at in range(0, hidden, step):
        w_in, w_back = in_ref[:, at : at + step], back_ref[at : at + step, :]
        pre = matmul(rows, w_in)
        d_active = matmul_t(grads, w_back)
        square = pre * pre
        wave = jnp.tanh(root * pre * (1.0 + 0.044715 * square))
        upper = 0.5 * (1.0 + wave)
        slope = upper + 0.5 * pre * (1.0 - wave * wave) * (
            root * (1.0 + 3 * 0.044715 * square)
        )
        active = (pre * upper).astype(BF16)
        d_gate = d_gate + jnp.sum(active.astype(F32) * d_active, axis=1, keepdims=True)
        d_pre = (gate * d_active * slope).astype(BF16)
        active_ref[:, at : at + step] = active
        d_pre_ref[:, at : at + step] = d_pre
        result = result + matmul(active, w_back)
        sent = sent + matmul_t(d_pre, w_in)
    result_ref[...] = result.astype(BF16)
    sent_ref[...] = sent.astype(BF16)
    sent_ref[:, :128] = (sent[:, :128] + lowered(d_gate, capacity)).astype(BF16)


def expert(capacity, rows, grads, w_in, w_back):
    count, width = rows.shape
    hidden = w_in.shape[1]
    step = min(count, max(256, capacity))
    by_rows = [pl.BlockSpec((step, size), lambda i: (i, 0)) for size in (width, hidden)]
    return pl.pallas_call(
        functools.partial(expert_kernel, capacity),
        grid=(count // step,),
        out_shape=[
            jax.ShapeDtypeStruct((count, hidden), BF16),
            jax.ShapeDtypeStruct((count, hidden), BF16),
            jax.ShapeDtypeStruct((count, width), BF16),
            jax.ShapeDtypeStruct((count, width), BF16),
            jax.ShapeDtypeStruct((count, width), BF16),
        ],
        in_specs=[
            by_rows[0],
            by_rows[0],
            pl.BlockSpec(w_in.shape, lambda i: (0, 0)),
            pl.BlockSpec(w_back.shape, lambda i: (0, 0)),
        ],
        out_specs=[by_rows[1], by_rows[1], by_rows[0], by_rows[0], by_rows[0]],
        compiler_params=pltpu.CompilerParams(vmem_limit_bytes=40 * 2**20),
        cost_estimate=pl.CostEstimate(
            flops=8 * count * width * hidden, bytes_accessed=2 * 10**7, transcendentals=count * hidden
        ),
    )(rows, grads, w_in, w_back)


def back_kernel(
    sizes,
    dims,
    both,
    cut,
    sent_ref,
    result_ref,
    dispatch_ref,
    gout_ref,
    tok_ref,
    n1_ref,
    proj_ref,
    chance_ref,
    mixed_ref,
    w_all,
    small_all,
    hidden_ref,
    n2_ref,
    router_ref,
    wout_ref,
    bucket_ref,
    layer_ref,
    gtok_ref,
    gqkv_ref,
    gout_w_ref,
    grouter_ref,
    gsmall_ref,
    att_all,
    dqkv,
    sums,
    part_out,
    part_in,
    comm,
    total_ref,
    chip_in,
    chip,
    row_in,
    column_in,
    row_sum,
    column_sum,
    deep,
    deep_in,
    returned,
    send,
    recv,
    all_sems,
):
    heads, experts, capacity, buckets = dims
    ys, xs, zs = sizes
    rows, width = tok_ref.shape
    half = width // 2
    seq = 2 * rows
    own_heads = heads // 2
    head = width // heads
    blocks = half // 128
    chunk_rows = comm.shape[2]
    rep, mine = lax.axis_index("rep"), lax.axis_index("shard")
    other = 1 - mine
    core = lax.rem(rep, 2)
    z = lax.rem(rep // 2, zs)
    x = lax.rem(rep // (2 * zs), xs)
    y = rep // (2 * zs * xs)

    def place(y_at, x_at, z_at, core_at):
        return ((y_at * xs + x_at) * zs + z_at) * 2 + core_at

    xp = [lax.rem(x + step, xs) for step in range(1, xs)]
    yp = [lax.rem(y + step, ys) for step in range(1, ys)]
    zp = [lax.rem(z + step, zs) for step in range(1, zs)]
    core_peer = (place(y, x, z, 1 - core), mine)
    x_peers = [(place(y, at, z, core), mine) for at in xp]
    y_peers = [(place(at, x, z, core), mine) for at in yp]
    z_peers = [(place(y, x, at, core), mine) for at in zp]
    peer = (rep, other)
    devices = 2 * experts
    me = 2 * rep + mine
    greet_all(devices)
    number = [0]

    def send_to(source, target, to):
        i = number[0]
        number[0] += 1
        copy = pltpu.make_async_remote_copy(
            source, target, send.at[i], recv.at[i], to, device_id_type=MESH
        )
        copy.start()
        return copy

    def finish(copies):
        for copy in copies:
            copy.wait()

    wide = sent_ref.shape[0]
    step = min(wide, max(256, capacity))
    d_gate = jnp.concatenate(
        [lifted(sent_ref[at : at + step, :128], capacity) for at in range(0, wide, step)], axis=0
    )
    shift = capacity.bit_length() - 1
    own_lane = (iota((wide, 128), 0) >> (shift + 1)) == iota((wide, 128), 1)
    d_gate = jnp.where(own_lane, d_gate, 0.0)
    dispatch = dispatch_ref[...]
    high, low = two_parts(d_gate)
    d_router = matmul(dispatch, high) + matmul(dispatch, low)
    router = router_ref[...]
    d_logits = router * (d_router - jnp.sum(router * d_router, axis=-1, keepdims=True))
    d_logits = d_logits.astype(BF16)
    d_n2 = matmul(dispatch, sent_ref[...]) + matmul_t(d_logits, router_weight(small_all, half))
    hidden = hidden_ref[...]
    factor = rms_factor(hidden)
    unit = hidden * factor
    scaled = d_n2 * gain_row(small_all, half, blocks)
    d_hidden = gout_ref[...].astype(F32) + factor * (
        scaled - unit * jnp.mean(scaled * unit, axis=-1, keepdims=True)
    )
    att_all[mine] = d_hidden.astype(BF16)
    shared = send_to(att_all.at[mine], att_all.at[mine], peer)
    send_blocks(lambda to: result_ref.at[to], returned, devices, all_sems.at[0], all_sems.at[1])
    own_block = pltpu.make_async_copy(result_ref.at[me], returned.at[me], all_sems.at[2])
    own_block.start()
    gtok_ref[...] = d_hidden
    g_gain_two = jnp.sum(d_n2 * unit, axis=0, keepdims=True)
    g_router = t_matmul(n2_ref[...], d_logits)

    def store(part, first, block):
        base = part * both
        span = both if part < 2 else chunk_rows - 2 * both
        at = 0
        while at < block.shape[0]:
            chunk_at, inside = divmod(first + at, span)
            count = min(span - inside, block.shape[0] - at)
            comm[chunk_at // 2, chunk_at % 2, base + inside : base + inside + count, :] = block[
                at : at + count
            ]
            at += count

    tile_rows = 3 * blocks * half
    for side in range(2):
        store(side, tile_rows, g_router[side * half : (side + 1) * half].astype(BF16))
    shared.wait()

    d_att = [att_all[0], att_all[1]]
    for block in range(2 * blocks):
        columns = slice(block * 128, (block + 1) * 128)
        grad = t_matmul(mixed_ref[:rows, :], d_att[0][:, columns])
        grad = grad + t_matmul(mixed_ref[rows:, :], d_att[1][:, columns])
        store(2, block * half, grad.astype(BF16))
    d_mixed = jnp.concatenate(
        [matmul_t(part, wout_ref[...]).astype(BF16) for part in d_att], axis=0
    )
    scale = head ** (-0.5)
    flip = (iota((seq, seq), 0) + iota((seq, seq), 1) == seq - 1).astype(F32).astype(BF16)
    for h in range(own_heads):
        at = h * head
        query = proj_ref[:, at : at + head]
        key = proj_ref[:, half + at : half + at + head]
        value = proj_ref[:, 2 * half + at : 2 * half + at + head]
        d_o = d_mixed[:, at : at + head]
        chance = chance_ref[h]
        d_chance = matmul_t(d_o, value)
        wide_chance = chance.astype(F32)
        inner = jnp.sum(wide_chance * d_chance, axis=-1, keepdims=True)
        d_scores = (wide_chance * (d_chance - inner)).astype(BF16)
        dqkv[:, at : at + head] = (matmul(d_scores, key) * scale).astype(BF16)
        dqkv[:, half + at : half + at + head] = (t_matmul(d_scores, query) * scale).astype(BF16)
        dqkv[:, 2 * half + at : 2 * half + at + head] = t_matmul(chance, d_o).astype(BF16)
        flipped = matmul(flip, d_scores)
        flipped = jnp.concatenate([flipped, jnp.zeros((seq, seq), F32)], axis=1)
        lined = pltpu.roll(flipped, 0, 1, stride=1, stride_axis=0)
        sums[pl.ds(mine * own_heads + h, 1), :] = jnp.sum(lined, axis=0, keepdims=True)
        sums[pl.ds(other * own_heads + h, 1), :] = jnp.zeros((1, 2 * seq), F32)

    theirs = pl.ds(pl.multiple_of(other * rows, 16), rows)
    ours = pl.ds(pl.multiple_of(mine * rows, 16), rows)

    def d_normed(which):
        return jnp.concatenate(
            [matmul_t(dqkv[which, :], w_all[side]) for side in range(2)], axis=1
        )

    part_out[...] = d_normed(theirs).astype(BF16)
    part_copy = send_to(part_out, part_in, peer)
    d_n1 = d_normed(ours)
    for block in range(3 * blocks):
        grad = t_matmul(n1_ref[...], dqkv[:, block * 128 : (block + 1) * 128]).astype(BF16)
        for side in range(2):
            store(side, block * half, grad[side * half : (side + 1) * half])
    levels = iota((buckets, 2 * seq), 0)
    one_hot = (levels == bucket_ref[...]).astype(F32).astype(BF16)
    high, low = two_parts(sums[...])
    g_table = (matmul_t(one_hot, high) + matmul_t(one_hot, low)).astype(BF16)
    for side in range(2):
        part = g_table[side * (buckets // 2) : (side + 1) * (buckets // 2)]
        store(side, tile_rows + half + 16, part)
    part_copy.wait()
    d_n1 = d_n1 + part_in[...].astype(F32)
    values = tok_ref[...].astype(F32)
    factor = rms_factor(values)
    unit = values * factor
    scaled = d_n1 * gain_row(small_all, half, 0)
    gtok_ref[...] = gtok_ref[...] + factor * (
        scaled - unit * jnp.mean(scaled * unit, axis=-1, keepdims=True)
    )
    g_gain_one = jnp.sum(d_n1 * unit, axis=0, keepdims=True)
    for side in range(2):
        pieces = [
            gain[:, side * half + i * 128 : side * half + (i + 1) * 128]
            for gain in (g_gain_one, g_gain_two)
            for i in range(blocks)
        ]
        pieces.append(jnp.zeros((16 - 2 * blocks, 128), F32))
        store(side, tile_rows + half, jnp.concatenate(pieces, axis=0).astype(BF16))

    first, second = pl.ds(0, cut), pl.ds(cut, chunk_rows - cut)
    chip_copy = send_to(comm.at[:, 1 - core], chip_in, core_peer)

    own_block.wait()
    wait_blocks(returned, devices, all_sems.at[0], all_sems.at[1])
    layer = hidden_ref[...]
    router_parts = two_parts(router_ref[...])
    per_step = step // capacity
    for i in range(wide // step):
        spread = (
            (iota((128, step), 1) + i * step) >> (shift + 1) == iota((128, step), 0)
        ).astype(F32).astype(BF16)
        weights = matmul(router_parts[0], spread) + matmul(router_parts[1], spread)
        weights = weights * dispatch_ref[:, i * step : (i + 1) * step].astype(F32)
        block = returned[i * per_step : (i + 1) * per_step].astype(F32)
        block = block.reshape(step, width).astype(BF16)
        for part in two_parts(weights):
            layer = layer + matmul(part, block)
    layer_ref[...] = layer.astype(BF16)
    finish([chip_copy])

    def add_chip(i, carry):
        total = comm[i, core].astype(F32) + chip_in[i].astype(F32)
        chip[i // (xs * zs), lax.rem(i // zs, xs), lax.rem(i, zs)] = total.astype(BF16)
        return carry

    lax.fori_loop(0, ys * xs * zs, add_chip, 0)
    copies = [
        send_to(chip.at[:, at, :, first], row_in.at[i], to)
        for i, (at, to) in enumerate(zip(xp, x_peers))
    ]
    copies += [
        send_to(chip.at[at, :, :, second], column_in.at[i], to)
        for i, (at, to) in enumerate(zip(yp, y_peers))
    ]
    finish(copies)

    def add_row(i, carry):
        for k in range(zs):
            total = chip[i, x, k, first].astype(F32)
            for j in range(xs - 1):
                total = total + row_in[j, i, k].astype(F32)
            row_sum[i, k] = total.astype(BF16)
        return carry

    def add_column(i, carry):
        for k in range(zs):
            total = chip[y, i, k, second].astype(F32)
            for j in range(ys - 1):
                total = total + column_in[j, i, k].astype(F32)
            column_sum[i, k] = total.astype(BF16)
        return carry

    lax.fori_loop(0, ys, add_row, 0)
    lax.fori_loop(0, xs, add_column, 0)
    copies = [
        send_to(row_sum.at[at], row_in.at[xs - 1 + i, 0], to)
        for i, (at, to) in enumerate(zip(yp, y_peers))
    ]
    copies += [
        send_to(column_sum.at[at], column_in.at[ys - 1 + i, 0], to)
        for i, (at, to) in enumerate(zip(xp, x_peers))
    ]
    finish(copies)
    for k in range(zs):
        total = row_sum[y, k].astype(F32)
        for i in range(ys - 1):
            total = total + row_in[xs - 1 + i, 0, k].astype(F32)
        deep[k, first] = total.astype(BF16)
        total = column_sum[x, k].astype(F32)
        for i in range(xs - 1):
            total = total + column_in[ys - 1 + i, 0, k].astype(F32)
        deep[k, second] = total.astype(BF16)
    finish([send_to(deep.at[at], deep_in.at[i], to) for i, (at, to) in enumerate(zip(zp, z_peers))])
    total = deep[z].astype(F32)
    for i in range(zs - 1):
        total = total + deep_in[i].astype(F32)
    done = total.astype(BF16)
    mine_at = pl.ds(pl.multiple_of(mine * both, 16), both)
    other_at = pl.ds(pl.multiple_of(other * both, 16), both)
    deep_in[zs - 1] = done
    out = total_ref.at[y, x, z, core]
    copies = [send_to(deep_in.at[zs - 1, other_at], out.at[mine_at], peer)]
    out[mine_at] = deep_in[zs - 1, mine_at]
    out[2 * both :] = done[2 * both :]
    finish(copies)
    finish([send_to(out, out, to) for to in z_peers])
    firsts = total_ref.at[y, x, :, core, first]
    seconds = total_ref.at[y, x, :, core, second]
    copies = [send_to(firsts, firsts, to) for to in y_peers]
    copies += [send_to(seconds, seconds, to) for to in x_peers]
    finish(copies)
    firsts = total_ref.at[:, x, :, core, first]
    seconds = total_ref.at[y, :, :, core, second]
    copies = [send_to(firsts, firsts, to) for to in x_peers]
    copies += [send_to(seconds, seconds, to) for to in y_peers]
    finish(copies)
    whole = total_ref.at[:, :, :, core]
    finish([send_to(whole, whole, core_peer)])

    def load(part, start, count):
        base = part * both
        span = both if part < 2 else chunk_rows - 2 * both
        pieces, at = [], 0
        while at < count:
            chunk_at, inside = divmod(start + at, span)
            size = min(span - inside, count - at)
            spot = (
                chunk_at // (2 * zs * xs),
                (chunk_at // (2 * zs)) % xs,
                (chunk_at // 2) % zs,
                chunk_at % 2,
            )
            pieces.append(total_ref[spot + (slice(base + inside, base + inside + size),)])
            at += size
        return pieces[0] if len(pieces) == 1 else jnp.concatenate(pieces, axis=0)

    for side in range(2):
        for block in range(3 * blocks):
            at = (block // blocks) * width + side * half + (block % blocks) * 128
            gqkv_ref[:, at : at + 128] = load(side, block * half, half)
    for block in range(2 * blocks):
        gout_w_ref[:, block * 128 : (block + 1) * 128] = load(2, block * half, half)
    grouter_ref[...] = sum(load(side, tile_rows, half).astype(F32) for side in range(2))
    gsmall_ref[...] = sum(
        load(side, tile_rows + half, 16 + buckets // 2).astype(F32) for side in range(2)
    )


def back(sizes, dims, sent, result, dispatch, cotangent, tokens, kept, w_out, bucket_row):
    ys, xs, zs = sizes
    heads, experts, capacity, buckets = dims
    rows, width = tokens.shape
    half, seq, lanes = width // 2, 2 * rows, 128
    count = 2 * ys * xs * zs
    both = up(3 * half * half // 128 + half + 16 + buckets // 2, 16 * count) // count
    chunk_rows = 2 * both + up(half * width // 128, 16 * count) // count
    cut = up(chunk_rows // 2, 16)
    per_core = count // 2
    many = 4 * (xs + ys) + 2 * zs + 4
    shapes = [
        ((rows, width), BF16),
        ((rows, width), F32),
        ((half, 3 * width), BF16),
        ((half, width), BF16),
        ((half, 128), F32),
        ((16 + buckets // 2, 128), F32),
    ]
    return pl.pallas_call(
        functools.partial(back_kernel, sizes, dims, both, cut),
        out_shape=[jax.ShapeDtypeStruct(*shape) for shape in shapes],
        in_specs=[VMEM_SPEC] * 16,
        out_specs=[VMEM_SPEC] * len(shapes),
        scratch_shapes=[
            pltpu.VMEM((2, rows, width), BF16),
            pltpu.VMEM((seq, 3 * half), BF16),
            pltpu.VMEM((128, 2 * seq), F32),
            pltpu.VMEM((rows, width), BF16),
            pltpu.VMEM((rows, width), BF16),
            pltpu.VMEM((per_core, 2, chunk_rows, lanes), BF16),
            pltpu.VMEM((ys, xs, zs, 2, chunk_rows, lanes), BF16),
            pltpu.VMEM((per_core, chunk_rows, lanes), BF16),
            pltpu.VMEM((ys, xs, zs, chunk_rows, lanes), BF16),
            pltpu.VMEM((xs + ys - 2, ys, zs, cut, lanes), BF16),
            pltpu.VMEM((xs + ys - 2, xs, zs, chunk_rows - cut, lanes), BF16),
            pltpu.VMEM((ys, zs, cut, lanes), BF16),
            pltpu.VMEM((xs, zs, chunk_rows - cut, lanes), BF16),
            pltpu.VMEM((zs, chunk_rows, lanes), BF16),
            pltpu.VMEM((zs, chunk_rows, lanes), BF16),
            pltpu.VMEM(result.shape, BF16),
            pltpu.SemaphoreType.DMA((many,)),
            pltpu.SemaphoreType.DMA((many,)),
            pltpu.SemaphoreType.DMA((3,)),
        ],
        compiler_params=pltpu.CompilerParams(
            collective_id=1, has_side_effects=True, vmem_limit_bytes=56 * 2**20
        ),
        cost_estimate=pl.CostEstimate(flops=60 * 10**9, bytes_accessed=2 * 10**8, transcendentals=0),
    )(sent, result, dispatch, cotangent, tokens, *kept, w_out, bucket_row)


def body(
    sizes,
    tokens,
    cotangent,
    attn_gain,
    w_qkv,
    w_out,
    rel_bias,
    buckets,
    ffn_gain,
    w_router,
    w_in,
    w_back,
    choice_ids,
):
    rows, width = tokens.shape
    half = width // 2
    bucket_half, heads = rel_bias.shape
    experts = w_router.shape[1]
    top = choice_ids.shape[1]
    capacity = up(max(2, 5 * rows * top // (4 * experts)) + 1, 8)
    slots = experts * capacity
    seq = 2 * rows
    dims = (heads, experts, capacity, 2 * bucket_half)
    blocks = half // 128

    flat_ids = choice_ids.reshape(-1)
    levels = jnp.arange(experts, dtype=jnp.int32)
    member = (flat_ids[:, None] == levels[None, :]).astype(BF16)
    order = jnp.arange(rows * top, dtype=jnp.int32)
    before = (order[:, None] > order[None, :]).astype(BF16)
    earlier = matmul(before, member)
    rank = jnp.sum(earlier * member.astype(F32), axis=1).astype(jnp.int32)
    slot = (flat_ids * capacity + rank).reshape(rows, top)
    dispatch = jnp.sum(
        (slot[:, :, None] == jnp.arange(slots, dtype=jnp.int32)).astype(BF16), axis=1
    )
    dispatch_two = jnp.broadcast_to(
        dispatch.reshape(rows, experts, 1, capacity), (rows, experts, 2, capacity)
    ).reshape(rows, 2 * slots)

    def swap_all(all_rows):
        blocks = all_rows.reshape(2 * experts, capacity, width)
        got = lax.all_to_all(blocks, ("rep", "shard"), split_axis=0, concat_axis=0, tiled=True)
        return got.reshape(2 * slots, width)

    gains = jnp.concatenate([attn_gain.reshape(blocks, 128), ffn_gain.reshape(blocks, 128)])
    small = jnp.concatenate(
        [
            jnp.pad(w_router, ((0, 0), (0, 128 - experts))),
            jnp.pad(gains, ((0, 16 - 2 * blocks), (0, 0))),
            jnp.pad(rel_bias, ((0, 0), (0, 128 - heads))),
        ]
    )
    nothing = jnp.full((seq,), -1, jnp.int32)
    back_order = buckets[::-1]
    bucket_front = jnp.concatenate([buckets[:1], nothing, back_order[:-1]]).reshape(1, 2 * seq)
    bucket_back = jnp.concatenate([back_order, nothing]).reshape(1, 2 * seq)
    *kept, arrived, grad_rows = front(
        sizes, dims, tokens, small, w_qkv, w_out, bucket_front, dispatch, cotangent
    )
    arrived, grad_rows = (block.reshape(2 * slots, width) for block in (arrived, grad_rows))

    expert_in, expert_back = w_in[0], w_back[0]
    activated, grad_pre, grad_arrived, result, grad_result = expert(
        capacity, arrived, grad_rows, expert_in, expert_back
    )
    sent = swap_all(grad_arrived)
    result = result.reshape(2 * experts, capacity, width)
    grad_back_expert = t_matmul(activated, grad_result)
    grad_in_expert = t_matmul(arrived, grad_pre)

    layer_out, grad_tokens, g_qkv, g_out, g_router, g_small = back(
        sizes, dims, sent, result, dispatch_two, cotangent, tokens, kept, w_out, bucket_back
    )

    return (
        layer_out,
        grad_tokens,
        g_small[:blocks].reshape(half),
        g_qkv.astype(F32),
        g_out.astype(F32),
        g_small[16:, :heads],
        g_small[blocks : 2 * blocks].reshape(half),
        g_router[:, :experts],
        grad_in_expert[None],
        grad_back_expert[None],
    )


SIZES = {64: (4, 4, 2), 4: (2, 1, 1), 8: (2, 2, 1)}


def solution(mesh):
    in_specs = (
        P(("rep", "shard"), None),
        P(("rep", "shard"), None),
        P("shard"),
        P("shard", None),
        P("shard", None),
        P("shard", None),
        P(),
        P("shard"),
        P("shard", None),
        P("rep", None, "shard"),
        P("rep", "shard", None),
        P(("rep", "shard"), None),
    )
    out_specs = (
        P(("rep", "shard"), None),
        P(("rep", "shard"), None),
        P("shard"),
        P("shard", None),
        P("shard", None),
        P("shard", None),
        P("shard"),
        P("shard", None),
        P("rep", None, "shard"),
        P("rep", "shard", None),
    )
    sizes = SIZES[mesh.shape["rep"]]
    return jax.shard_map(
        functools.partial(body, sizes),
        mesh=mesh,
        in_specs=in_specs,
        out_specs=out_specs,
        check_vma=False,
    )
```

profile of v0, /device:TPU:1, one launch (start us, length us, event | category | flops | bytes accessed | tf_op | source)
XLA Modules:
  0.0 245.8 jit_solution(5539474274370632612)
XLA Ops:
  0.6 1.2 slice.21
  3.5 0.9 copy.40
  8.1 1.1 copy-done.2
  9.2 1.0 copy-done.3
  10.1 1.0 copy-done.4
  11.1 75.2 %shard_map.195 = (bf16[384,768]{1,0:T(8,128)(2,1)S(1)}, bf16[384,1152]{1,0:T(8,128)(2,1)S(1)}, bf16[6,384,384]{2,1,0:T(8,128)(2,1)}, bf16[384,384]{1,0:T(8,128)(...) custom-call(bf16[192,768]{1,0:T(8,128)(2,1)S(1)} %copy-done.3, ...), custom_call_target="tpu_custom_call" | custom-call | flops 30000001024 | bytes 100000000 | tf_op jit(solution)/shard_map/pallas_call | solution.py:339
  86.3 0.9 copy-done.7
  88.1 1.9 copy-done.6
  90.0 12.8 %shard_map.196 = (bf16[1024,1536]{1,0:T(8,128)(2,1)}, bf16[1024,1536]{1,0:T(8,128)(2,1)}, bf16[1024,768]{1,0:T(8,128)(2,1)}, bf16[1024,768]{1,0:T(8,128)(2,1)S(1)}, bf16[1024,768]{1,0:T(8,128)(2,1)S(1)}) custom-call(bf16[1024,768]{1,0:T(8,128)(2,1)S(1)} %bitcast.26, bf16[1024,768]{1,0:T(8,128)(2,1)S(1)} %bitcast.30, bf16[768,1536]{1,0:T(8,128)(2,1)S(1)} %bitcast.27, ...), custom_call_target="tpu_custom_call" | custom-call | flops 9663676416 | bytes 20000000 | tf_op jit(solution)/shard_map/pallas_call | solution.py:409
  102.8 1.2 copy-done.5
  104.0 7.3 %all-to-all-start = ((bf16[128,8,768]{2,1,0:T(8,128)(2,1)}), bf16[128,8,768]{2,1,0:T(8,128)(2,1)}, u32[]{:S(2)}, u32[]{:S(2)}) async-start(bf16[128,8,768]{2,1,0:T(8,128)(2,1)} %bitcast.6), calls=%async_computation | async-start | bytes 3145728 | tf_op jit(solution)/shard_map/all_to_all | solution.py:869
  111.4 0.8 copy.43
  112.9 1.8 broadcast_in_dim.22
  114.6 2.0 copy.44.dispatch_ref
  116.6 6.3 %convolution_bitcast_fusion.1 = f32[1,768,1536]{2,1,0:T(8,128)} fusion(bf16[1024,1536]{1,0:T(8,128)(2,1)} %get-tuple-element.51, bf16[128,8,768]{2,1,0:T(8,128)(2,1)S(1)} %get-tuple-element.32), kind=kOutput, calls=%fused_computation.1 | convolution fusion | flops 2415919104 | bytes 9437184 | tf_op jit(solution)/shard_map/dot_general | solution.py:75
  122.9 4.3 %convolution_bitcast_fusion = f32[1,1536,768]{2,1,0:T(8,128)} fusion(bf16[1024,1536]{1,0:T(8,128)(2,1)S(1)} %copy-done.18, bf16[1024,768]{1,0:T(8,128)(2,1)S(1)} %get-tuple-element.53), kind=kOutput, calls=%fused_computation | convolution fusion | flops 2415919104 | bytes 9437184 | tf_op jit(solution)/shard_map/dot_general | solution.py:75
  127.2 8.3 %all-to-all-done = bf16[128,8,768]{2,1,0:T(8,128)(2,1)} async-done(((bf16[128,8,768]{2,1,0:T(8,128)(2,1)}), bf16[128,8,768]{2,1,0:T(8,128)(2,1)}, u32[]{:S(2)}, u32[]{:S(2)}) %all-to-all-start) | async-done | bytes 1572896 | tf_op jit(solution)/shard_map/all_to_all | solution.py:869
  135.5 100.2 %shard_map.197 = (bf16[192,768]{1,0:T(8,128)(2,1)}, f32[192,768]{1,0:T(8,128)}, bf16[384,2304]{1,0:T(8,128)(2,1)}, bf16[384,768]{1,0:T(8,128)(2,1)}, f32[384,128]{1,0:T(8,128)}, /*index=5*/f32[32,128]{1,0:T(8,128)}) custom-call(bf16[1024,768]{1,0:T(8,128)(2,1)} %bitcast.7.sent_ref, bf16[128,8,768]{2,1,0:T(8,128)(2,1)} %bitcast.29, ...), custom_call_target="tpu_custom_call" | custom-call | flops 60000002048 | bytes 200000000 | tf_op jit(solution)/shard_map/pallas_call | solution.py:793
  235.7 1.4 slice_bitcast_fusion
  237.1 1.3 slice.25
  238.4 1.7 copy.45
  240.1 2.2 convert_element_type.38
  242.3 2.0 convert_element_type.37
  245.0 0.8 copy.49
  (52 shorter events, 7.6 us)
Async XLA Ops:
  8.1 1.1 copy-start.2
  9.1 1.0 copy-start.3
  10.1 1.0 copy-start.4
  11.1 77.0 %copy-start = (bf16[1,768,1536]{2,1,0:T(8,128)(2,1)S(1)}, bf16[1,768,1536]{2,1,0:T(8,128)(2,1)}, u32[]{:S(2)}) copy-start(bf16[1,768,1536]{2,1,0:T(8,128)(2,1)} %param.21) | copy-start | bytes 7077892
  11.1 77.0 %copy-start.1 = (bf16[1,1536,768]{2,1,0:T(8,128)(2,1)S(1)}, bf16[1,1536,768]{2,1,0:T(8,128)(2,1)}, u32[]{:S(2)}) copy-start(bf16[1,1536,768]{2,1,0:T(8,128)(2,1)} %param.22) | copy-start | bytes 7077892
  86.3 0.9 copy-start.7
  87.2 0.8 copy-start.8
  88.0 14.7 %copy-start.9 = (f32[192,768]{1,0:T(8,128)}, f32[192,768]{1,0:T(8,128)S(1)}, u32[]{:S(2)}) copy-start(f32[192,768]{1,0:T(8,128)S(1)} %get-tuple-element.42.hidden_ref) | copy-start | bytes 1769476
  88.0 14.7 %copy-start.10 = (bf16[384,384]{1,0:T(8,128)(2,1)}, bf16[384,384]{1,0:T(8,128)(2,1)S(1)}, u32[]{:S(2)}) copy-start(bf16[384,384]{1,0:T(8,128)(2,1)S(1)} %get-tuple-element.39.mixed_ref) | copy-start | bytes 884740
  88.0 14.7 %copy-start.11 = (bf16[192,768]{1,0:T(8,128)(2,1)}, bf16[192,768]{1,0:T(8,128)(2,1)S(1)}, u32[]{:S(2)}) copy-start(bf16[192,768]{1,0:T(8,128)(2,1)S(1)} %get-tuple-element.43.n2_ref) | copy-start | bytes 884740
  88.0 14.7 %copy-start.12 = (bf16[2,416,128]{2,1,0:T(8,128)(2,1)}, bf16[2,416,128]{2,1,0:T(8,128)(2,1)S(1)}, u32[]{:S(2)}) copy-start(bf16[2,416,128]{2,1,0:T(8,128)(2,1)S(1)} %get-tuple-element.41.small_all) | copy-start | bytes 638980
  88.0 14.7 %copy-start.13 = (f32[192,128]{1,0:T(8,128)}, f32[192,128]{1,0:T(8,128)S(1)}, u32[]{:S(2)}) copy-start(f32[192,128]{1,0:T(8,128)S(1)} %get-tuple-element.44.router_ref) | copy-start | bytes 294916
  88.1 1.9 copy-start.6
  102.8 1.2 copy-start.5
  104.0 7.3 %copy-start.17 = (s32[384]{0:T(512)S(1)}, s32[384]{0:T(512)}, u32[]{:S(2)}) copy-start(s32[384]{0:T(512)} %param.18) | copy-start | bytes 4612
  104.0 31.5 %all-to-all-start = ((bf16[128,8,768]{2,1,0:T(8,128)(2,1)}), bf16[128,8,768]{2,1,0:T(8,128)(2,1)}, u32[]{:S(2)}, u32[]{:S(2)}) async-start(bf16[128,8,768]{2,1,0:T(8,128)(2,1)} %bitcast.6), calls=%async_computation | async-start | bytes 3145728 | tf_op jit(solution)/shard_map/all_to_all | solution.py:869
  116.6 6.3 %copy-start.18 = (bf16[1024,1536]{1,0:T(8,128)(2,1)S(1)}, bf16[1024,1536]{1,0:T(8,128)(2,1)}, u32[]{:S(2)}) copy-start(bf16[1024,1536]{1,0:T(8,128)(2,1)} %get-tuple-element.52) | copy-start | bytes 9437188
  235.7 6.5 %copy-start.14 = (bf16[384,2304]{1,0:T(8,128)(2,1)S(1)}, bf16[384,2304]{1,0:T(8,128)(2,1)}, u32[]{:S(2)}) copy-start(bf16[384,2304]{1,0:T(8,128)(2,1)} %get-tuple-element.48) | copy-start | bytes 5308420
  242.3 2.0 copy-start.16
  242.3 2.7 %copy-start.15 = (f32[192,768]{1,0:T(8,128)S(1)}, f32[192,768]{1,0:T(8,128)}, u32[]{:S(2)}) copy-start(f32[192,768]{1,0:T(8,128)} %get-tuple-element.107) | copy-start | bytes 1769476
where the time goes:
time: 247 us; the launch traced here: 246 us
  Pallas kernels  188 us (76%)
  local copies, waits for them, and re-layouts  23.3 us (9%)
  matrix products  10.8 us (4%)
  waiting for transfers between devices  8.26 us (3%)
  starting transfers between devices  7.32 us (3%)
  other arithmetic  7.16 us (3%)
    pallas_call x1, Pallas kernels, back(): pl.pallas_call(functools.partial(back_kernel, sizes, dims, both, cut), ou...  100 us
    pallas_call x1, Pallas kernels, front(): pl.pallas_call(functools.partial(front_kernel, sizes, dims), out_shape=[j...  75.2 us
    unnamed x45, local copies, waits for them, and re-layouts  13 us
    pallas_call x1, Pallas kernels, expert(): pl.pallas_call(functools.partial(expert_kernel, capacity), grid=(count //...  12.8 us
    dot_general x3, matrix products, dot(): lax.dot_general(a, b, (contract, ((), ())), preferred_element_type=F32)  10.8 us
    all_to_all x1, waiting for transfers between devices, swap_all(): lax.all_to_all(blocks, ('rep', 'shard'), split_axis=0, concat_axis=0, til...  8.26 us
    all_to_all x1, starting transfers between devices, swap_all(): lax.all_to_all(blocks, ('rep', 'shard'), split_axis=0, concat_axis=0, til...  7.32 us
  transfers between devices with their start and end apart: 1, of which 1 were waited for; matrix products, arithmetic and copies ran while one was open for 6% of the time, Pallas kernels for 0%

commit v1 on v0

--- a/solution.py
+++ b/solution.py
@@ -236,16 +236,16 @@
     dispatch = dispatch_ref[...]
     blocks = t_matmul(dispatch, gout_ref[...]).reshape(experts, capacity, width)
     outgoing_grads[...] = blocks.astype(BF16)
+    send_blocks(
+        lambda to: outgoing_grads.at[to // 2], grad_rows_ref, devices, send.at[10], recv.at[10]
+    )
+    own_block = pltpu.make_async_copy(outgoing_grads.at[rep], grad_rows_ref.at[me], local.at[0])
+    own_block.start()
 
     for copy in weight_copies:
         copy.wait()
     got = w_all.at[other, pl.ds(pl.multiple_of(core * (half // 2), 16), half // 2)]
     passed = remote(8, got, got, core_peer)
-    send_blocks(
-        lambda to: outgoing_grads.at[to // 2], grad_rows_ref, devices, send.at[10], recv.at[10]
-    )
-    own_block = pltpu.make_async_copy(outgoing_grads.at[rep], grad_rows_ref.at[me], local.at[0])
-    own_block.start()
     tok_copy.wait()
     for side in range(2):
         values = tok_all[side].astype(F32)
@@ -433,8 +433,7 @@
 def back_kernel(
     sizes,
     dims,
-    both,
-    cut,
+    cuts,
     sent_ref,
     result_ref,
     dispatch_ref,
@@ -462,20 +461,11 @@
     sums,
     part_out,
     part_in,
-    comm,
-    total_ref,
-    chip_in,
-    chip,
-    row_in,
-    column_in,
-    row_sum,
-    column_sum,
-    deep,
-    deep_in,
     returned,
     send,
     recv,
     all_sems,
+    *scratch,
 ):
     heads, experts, capacity, buckets = dims
     ys, xs, zs = sizes
@@ -485,7 +475,7 @@
     own_heads = heads // 2
     head = width // heads
     blocks = half // 128
-    chunk_rows = comm.shape[2]
+    sets = [scratch[10 * i : 10 * i + 10] for i in range(3)]
     rep, mine = lax.axis_index("rep"), lax.axis_index("shard")
     other = 1 - mine
     core = lax.rem(rep, 2)
@@ -553,21 +543,129 @@
     g_gain_two = jnp.sum(d_n2 * unit, axis=0, keepdims=True)
     g_router = t_matmul(n2_ref[...], d_logits)
 
-    def store(part, first, block):
-        base = part * both
-        span = both if part < 2 else chunk_rows - 2 * both
-        at = 0
+    def span_of(which):
+        both, n = cuts[which]
+        return both if both else n
+
+    def store(which, side, first, block):
+        span, at = span_of(which), 0
+        base = side * span
         while at < block.shape[0]:
             chunk_at, inside = divmod(first + at, span)
             count = min(span - inside, block.shape[0] - at)
-            comm[chunk_at // 2, chunk_at % 2, base + inside : base + inside + count, :] = block[
-                at : at + count
-            ]
+            sets[which][0][
+                chunk_at // 2, chunk_at % 2, base + inside : base + inside + count, :
+            ] = block[at : at + count]
             at += count
 
-    tile_rows = 3 * blocks * half
+    def replica_sum(which):
+        comm, total_ref, chip_in, chip, row_in, column_in, row_sum, column_sum, deep, deep_in = (
+            sets[which]
+        )
+        both, n = cuts[which]
+        cut = up(n // 2, 16)
+        first, second = pl.ds(0, cut), pl.ds(cut, n - cut)
+        copies = [send_to(comm.at[:, 1 - core], chip_in, core_peer)]
+        yield
+        finish(copies)
+
+        def add_chip(i, carry):
+            total = comm[i, core].astype(F32) + chip_in[i].astype(F32)
+            chip[i // (xs * zs), lax.rem(i // zs, xs), lax.rem(i, zs)] = total.astype(BF16)
+            return carry
+
+        lax.fori_loop(0, ys * xs * zs, add_chip, 0)
+        copies = [
+            send_to(chip.at[:, at, :, first], row_in.at[i], to)
+            for i, (at, to) in enumerate(zip(xp, x_peers))
+        ]
+        copies += [
+            send_to(chip.at[at, :, :, second], column_in.at[i], to)
+            for i, (at, to) in enumerate(zip(yp, y_peers))
+        ]
+        yield
+        finish(copies)
+
+        def add_row(i, carry):
+            for k in range(zs):
+                total = chip[i, x, k, first].astype(F32)
+                for j in range(xs - 1):
+                    total = total + row_in[j, i, k].astype(F32)
+                row_sum[i, k] = total.astype(BF16)
+            return carry
+
+        def add_column(i, carry):
+            for k in range(zs):
+                total = chip[y, i, k, second].astype(F32)
+                for j in range(ys - 1):
+                    total = total + column_in[j, i, k].astype(F32)
+                column_sum[i, k] = total.astype(BF16)
+            return carry
+
+        lax.fori_loop(0, ys, add_row, 0)
+        lax.fori_loop(0, xs, add_column, 0)
+        copies = [
+            send_to(row_sum.at[at], row_in.at[xs - 1 + i, 0], to)
+            for i, (at, to) in enumerate(zip(yp, y_peers))
+        ]
+        copies += [
+            send_to(column_sum.at[at], column_in.at[ys - 1 + i, 0], to)
+            for i, (at, to) in enumerate(zip(xp, x_peers))
+        ]
+        yield
+        finish(copies)
+        for k in range(zs):
+            total = row_sum[y, k].astype(F32)
+            for i in range(ys - 1):
+                total = total + row_in[xs - 1 + i, 0, k].astype(F32)
+            deep[k, first] = total.astype(BF16)
+            total = column_sum[x, k].astype(F32)
+            for i in range(xs - 1):
+                total = total + column_in[ys - 1 + i, 0, k].astype(F32)
+            deep[k, second] = total.astype(BF16)
+        copies = [
+            send_to(deep.at[at], deep_in.at[i], to) for i, (at, to) in enumerate(zip(zp, z_peers))
+        ]
+        yield
+        finish(copies)
+        total = deep[z].astype(F32)
+        for i in range(zs - 1):
+            total = total + deep_in[i].astype(F32)
+        deep_in[zs - 1] = total.astype(BF16)
+        out = total_ref.at[y, x, z, core]
+        if both:
+            mine_at = pl.ds(pl.multiple_of(mine * both, 16), both)
+            other_at = pl.ds(pl.multiple_of(other * both, 16), both)
+            copies = [send_to(deep_in.at[zs - 1, other_at], out.at[mine_at], peer)]
+            out[mine_at] = deep_in[zs - 1, mine_at]
+            yield
+            finish(copies)
+        else:
+            out[...] = deep_in[zs - 1]
+        copies = [send_to(out, out, to) for to in z_peers]
+        yield
+        finish(copies)
+        firsts = total_ref.at[y, x, :, core, first]
+        seconds = total_ref.at[y, x, :, core, second]
+        copies = [send_to(firsts, firsts, to) for to in y_peers]
+        copies += [send_to(seconds, seconds, to) for to in x_peers]
+        yield
+        finish(copies)
+        firsts = total_ref.at[:, x, :, core, first]
+        seconds = total_ref.at[y, :, :, core, second]
+        copies = [send_to(firsts, firsts, to) for to in x_peers]
+        copies += [send_to(seconds, seconds, to) for to in y_peers]
+        yield
+        finish(copies)
+        whole = total_ref.at[:, :, :, core]
+        copies = [send_to(whole, whole, core_peer)]
+        yield
+        finish(copies)
+
+    early = -(-5 * 3 * blocks // 9)
+    tile_rows = (3 * blocks - early) * half
     for side in range(2):
-        store(side, tile_rows, g_router[side * half : (side + 1) * half].astype(BF16))
+        store(1, side, tile_rows, g_router[side * half : (side + 1) * half].astype(BF16))
     shared.wait()
 
     d_att = [att_all[0], att_all[1]]
@@ -575,7 +673,9 @@
         columns = slice(block * 128, (block + 1) * 128)
         grad = t_matmul(mixed_ref[:rows, :], d_att[0][:, columns])
         grad = grad + t_matmul(mixed_ref[rows:, :], d_att[1][:, columns])
-        store(2, block * half, grad.astype(BF16))
+        store(2, 0, block * half, grad.astype(BF16))
+    sum_out = replica_sum(2)
+    next(sum_out, None)
     d_mixed = jnp.concatenate(
         [matmul_t(part, wout_ref[...]).astype(BF16) for part in d_att], axis=0
     )
@@ -600,6 +700,7 @@
         lined = pltpu.roll(flipped, 0, 1, stride=1, stride_axis=0)
         sums[pl.ds(mine * own_heads + h, 1), :] = jnp.sum(lined, axis=0, keepdims=True)
         sums[pl.ds(other * own_heads + h, 1), :] = jnp.zeros((1, 2 * seq), F32)
+        next(sum_out, None)
 
     theirs = pl.ds(pl.multiple_of(other * rows, 16), rows)
     ours = pl.ds(pl.multiple_of(mine * rows, 16), rows)
@@ -612,17 +713,27 @@
     part_out[...] = d_normed(theirs).astype(BF16)
     part_copy = send_to(part_out, part_in, peer)
     d_n1 = d_normed(ours)
-    for block in range(3 * blocks):
-        grad = t_matmul(n1_ref[...], dqkv[:, block * 128 : (block + 1) * 128]).astype(BF16)
-        for side in range(2):
-            store(side, block * half, grad[side * half : (side + 1) * half])
+
+    def weight_blocks(which, chosen):
+        for i, block in enumerate(chosen):
+            grad = t_matmul(n1_ref[...], dqkv[:, block * 128 : (block + 1) * 128]).astype(BF16)
+            for side in range(2):
+                store(which, side, i * half, grad[side * half : (side + 1) * half])
+
+    weight_blocks(0, range(early))
+    sum_early = replica_sum(0)
+    next(sum_early, None)
+    next(sum_out, None)
+    weight_blocks(1, range(early, 3 * blocks))
+    next(sum_early, None)
+    next(sum_out, None)
     levels = iota((buckets, 2 * seq), 0)
     one_hot = (levels == bucket_ref[...]).astype(F32).astype(BF16)
     high, low = two_parts(sums[...])
     g_table = (matmul_t(one_hot, high) + matmul_t(one_hot, low)).astype(BF16)
     for side in range(2):
         part = g_table[side * (buckets // 2) : (side + 1) * (buckets // 2)]
-        store(side, tile_rows + half + 16, part)
+        store(1, side, tile_rows + half + 16, part)
     part_copy.wait()
     d_n1 = d_n1 + part_in[...].astype(F32)
     values = tok_ref[...].astype(F32)
@@ -640,10 +751,12 @@
             for i in range(blocks)
         ]
         pieces.append(jnp.zeros((16 - 2 * blocks, 128), F32))
-        store(side, tile_rows + half, jnp.concatenate(pieces, axis=0).astype(BF16))
-
-    first, second = pl.ds(0, cut), pl.ds(cut, chunk_rows - cut)
-    chip_copy = send_to(comm.at[:, 1 - core], chip_in, core_peer)
+        store(1, side, tile_rows + half, jnp.concatenate(pieces, axis=0).astype(BF16))
+
+    sum_late = replica_sum(1)
+    next(sum_late, None)
+    next(sum_early, None)
+    next(sum_late, None)
 
     own_block.wait()
     wait_blocks(returned, devices, all_sems.at[0], all_sems.at[1])
@@ -661,90 +774,13 @@
         for part in two_parts(weights):
             layer = layer + matmul(part, block)
     layer_ref[...] = layer.astype(BF16)
-    finish([chip_copy])
-
-    def add_chip(i, carry):
-        total = comm[i, core].astype(F32) + chip_in[i].astype(F32)
-        chip[i // (xs * zs), lax.rem(i // zs, xs), lax.rem(i, zs)] = total.astype(BF16)
-        return carry
-
-    lax.fori_loop(0, ys * xs * zs, add_chip, 0)
-    copies = [
-        send_to(chip.at[:, at, :, first], row_in.at[i], to)
-        for i, (at, to) in enumerate(zip(xp, x_peers))
-    ]
-    copies += [
-        send_to(chip.at[at, :, :, second], column_in.at[i], to)
-        for i, (at, to) in enumerate(zip(yp, y_peers))
-    ]
-    finish(copies)
-
-    def add_row(i, carry):
-        for k in range(zs):
-            total = chip[i, x, k, first].astype(F32)
-            for j in range(xs - 1):
-                total = total + row_in[j, i, k].astype(F32)
-            row_sum[i, k] = total.astype(BF16)
-        return carry
-
-    def add_column(i, carry):
-        for k in range(zs):
-            total = chip[y, i, k, second].astype(F32)
-            for j in range(ys - 1):
-                total = total + column_in[j, i, k].astype(F32)
-            column_sum[i, k] = total.astype(BF16)
-        return carry
-
-    lax.fori_loop(0, ys, add_row, 0)
-    lax.fori_loop(0, xs, add_column, 0)
-    copies = [
-        send_to(row_sum.at[at], row_in.at[xs - 1 + i, 0], to)
-        for i, (at, to) in enumerate(zip(yp, y_peers))
-    ]
-    copies += [
-        send_to(column_sum.at[at], column_in.at[ys - 1 + i, 0], to)
-        for i, (at, to) in enumerate(zip(xp, x_peers))
-    ]
-    finish(copies)
-    for k in range(zs):
-        total = row_sum[y, k].astype(F32)
-        for i in range(ys - 1):
-            total = total + row_in[xs - 1 + i, 0, k].astype(F32)
-        deep[k, first] = total.astype(BF16)
-        total = column_sum[x, k].astype(F32)
-        for i in range(xs - 1):
-            total = total + column_in[ys - 1 + i, 0, k].astype(F32)
-        deep[k, second] = total.astype(BF16)
-    finish([send_to(deep.at[at], deep_in.at[i], to) for i, (at, to) in enumerate(zip(zp, z_peers))])
-    total = deep[z].astype(F32)
-    for i in range(zs - 1):
-        total = total + deep_in[i].astype(F32)
-    done = total.astype(BF16)
-    mine_at = pl.ds(pl.multiple_of(mine * both, 16), both)
-    other_at = pl.ds(pl.multiple_of(other * both, 16), both)
-    deep_in[zs - 1] = done
-    out = total_ref.at[y, x, z, core]
-    copies = [send_to(deep_in.at[zs - 1, other_at], out.at[mine_at], peer)]
-    out[mine_at] = deep_in[zs - 1, mine_at]
-    out[2 * both :] = done[2 * both :]
-    finish(copies)
-    finish([send_to(out, out, to) for to in z_peers])
-    firsts = total_ref.at[y, x, :, core, first]
-    seconds = total_ref.at[y, x, :, core, second]
-    copies = [send_to(firsts, firsts, to) for to in y_peers]
-    copies += [send_to(seconds, seconds, to) for to in x_peers]
-    finish(copies)
-    firsts = total_ref.at[:, x, :, core, first]
-    seconds = total_ref.at[y, :, :, core, second]
-    copies = [send_to(firsts, firsts, to) for to in x_peers]
-    copies += [send_to(seconds, seconds, to) for to in y_peers]
-    finish(copies)
-    whole = total_ref.at[:, :, :, core]
-    finish([send_to(whole, whole, core_peer)])
-
-    def load(part, start, count):
-        base = part * both
-        span = both if part < 2 else chunk_rows - 2 * both
+    for _ in range(10):
+        for running in (sum_out, sum_early, sum_late):
+            next(running, None)
+
+    def load(which, side, start, count):
+        span = span_of(which)
+        base = side * span
         pieces, at = [], 0
         while at < count:
             chunk_at, inside = divmod(start + at, span)
@@ -755,19 +791,20 @@
                 (chunk_at // 2) % zs,
                 chunk_at % 2,
             )
-            pieces.append(total_ref[spot + (slice(base + inside, base + inside + size),)])
+            pieces.append(sets[which][1][spot + (slice(base + inside, base + inside + size),)])
             at += size
         return pieces[0] if len(pieces) == 1 else jnp.concatenate(pieces, axis=0)
 
     for side in range(2):
         for block in range(3 * blocks):
             at = (block // blocks) * width + side * half + (block % blocks) * 128
-            gqkv_ref[:, at : at + 128] = load(side, block * half, half)
+            which, i = (0, block) if block < early else (1, block - early)
+            gqkv_ref[:, at : at + 128] = load(which, side, i * half, half)
     for block in range(2 * blocks):
-        gout_w_ref[:, block * 128 : (block + 1) * 128] = load(2, block * half, half)
-    grouter_ref[...] = sum(load(side, tile_rows, half).astype(F32) for side in range(2))
+        gout_w_ref[:, block * 128 : (block + 1) * 128] = load(2, 0, block * half, half)
+    grouter_ref[...] = sum(load(1, side, tile_rows, half).astype(F32) for side in range(2))
     gsmall_ref[...] = sum(
-        load(side, tile_rows + half, 16 + buckets // 2).astype(F32) for side in range(2)
+        load(1, side, tile_rows + half, 16 + buckets // 2).astype(F32) for side in range(2)
     )
 
 
@@ -777,11 +814,29 @@
     rows, width = tokens.shape
     half, seq, lanes = width // 2, 2 * rows, 128
     count = 2 * ys * xs * zs
-    both = up(3 * half * half // 128 + half + 16 + buckets // 2, 16 * count) // count
-    chunk_rows = 2 * both + up(half * width // 128, 16 * count) // count
-    cut = up(chunk_rows // 2, 16)
+    blocks = half // 128
+    early = -(-5 * 3 * blocks // 9)
+    late_rows = (3 * blocks - early) * half + half + 16 + buckets // 2
+    both = [up(length, 16 * count) // count for length in (early * half, late_rows)]
+    last = up(half * width // 128, 16 * count) // count
+    cuts = [(both[0], 2 * both[0]), (both[1], 2 * both[1]), (0, last)]
     per_core = count // 2
-    many = 4 * (xs + ys) + 2 * zs + 4
+    many = 3 * (4 * (xs + ys) + 2 * zs + 4)
+    landing = []
+    for _, n in cuts:
+        cut = up(n // 2, 16)
+        landing += [
+            (per_core, 2, n, lanes),
+            (ys, xs, zs, 2, n, lanes),
+            (per_core, n, lanes),
+            (ys, xs, zs, n, lanes),
+            (xs + ys - 2, ys, zs, cut, lanes),
+            (xs + ys - 2, xs, zs, n - cut, lanes),
+            (ys, zs, cut, lanes),
+            (xs, zs, n - cut, lanes),
+            (zs, n, lanes),
+            (zs, n, lanes),
+        ]
     shapes = [
         ((rows, width), BF16),
         ((rows, width), F32),
@@ -791,7 +846,7 @@
         ((16 + buckets // 2, 128), F32),
     ]
     return pl.pallas_call(
-        functools.partial(back_kernel, sizes, dims, both, cut),
+        functools.partial(back_kernel, sizes, dims, cuts),
         out_shape=[jax.ShapeDtypeStruct(*shape) for shape in shapes],
         in_specs=[VMEM_SPEC] * 16,
         out_specs=[VMEM_SPEC] * len(shapes),
@@ -801,21 +856,12 @@
             pltpu.VMEM((128, 2 * seq), F32),
             pltpu.VMEM((rows, width), BF16),
             pltpu.VMEM((rows, width), BF16),
-            pltpu.VMEM((per_core, 2, chunk_rows, lanes), BF16),
-            pltpu.VMEM((ys, xs, zs, 2, chunk_rows, lanes), BF16),
-            pltpu.VMEM((per_core, chunk_rows, lanes), BF16),
-            pltpu.VMEM((ys, xs, zs, chunk_rows, lanes), BF16),
-            pltpu.VMEM((xs + ys - 2, ys, zs, cut, lanes), BF16),
-            pltpu.VMEM((xs + ys - 2, xs, zs, chunk_rows - cut, lanes), BF16),
-            pltpu.VMEM((ys, zs, cut, lanes), BF16),
-            pltpu.VMEM((xs, zs, chunk_rows - cut, lanes), BF16),
-            pltpu.VMEM((zs, chunk_rows, lanes), BF16),
-            pltpu.VMEM((zs, chunk_rows, lanes), BF16),
             pltpu.VMEM(result.shape, BF16),
             pltpu.SemaphoreType.DMA((many,)),
             pltpu.SemaphoreType.DMA((many,)),
             pltpu.SemaphoreType.DMA((3,)),
-        ],
+        ]
+        + [pltpu.VMEM(shape, BF16) for shape in landing],
         compiler_params=pltpu.CompilerParams(
             collective_id=1, has_side_effects=True, vmem_limit_bytes=56 * 2**20
         ),

time: 247 us -> 253 us (1.024)
  Pallas kernels: 188 us -> 195 us
    pallas_call x1, Pallas kernels: 100 us -> 104 us  [back(): pl.pallas_call(functools.partial(back_kernel, sizes, dims, cuts), out_sha...]
    pallas_call x1, Pallas kernels: 75.2 us -> 78.8 us  [front(): pl.pallas_call(functools.partial(front_kernel, sizes, dims), out_shape=[j...]
where the time goes in v1:
time: 253 us; the launch traced here: 252 us
  Pallas kernels  195 us (77%)
  local copies, waits for them, and re-layouts  23.3 us (9%)
  matrix products  10.8 us (4%)
  waiting for transfers between devices  8.26 us (3%)
  other arithmetic  7.16 us (3%)
  starting transfers between devices  6.28 us (2%)
    pallas_call x1, Pallas kernels, back(): pl.pallas_call(functools.partial(back_kernel, sizes, dims, cuts), out_sha...  104 us
    pallas_call x1, Pallas kernels, front(): pl.pallas_call(functools.partial(front_kernel, sizes, dims), out_shape=[j...  78.8 us
    unnamed x45, local copies, waits for them, and re-layouts  13 us
    pallas_call x1, Pallas kernels, expert(): pl.pallas_call(functools.partial(expert_kernel, capacity), grid=(count //...  12.8 us
    dot_general x3, matrix products, dot(): lax.dot_general(a, b, (contract, ((), ())), preferred_element_type=F32)  10.8 us
    all_to_all x1, waiting for transfers between devices, swap_all(): lax.all_to_all(blocks, ('rep', 'shard'), split_axis=0, concat_axis=0, til...  8.26 us
    all_to_all x1, starting transfers between devices, swap_all(): lax.all_to_all(blocks, ('rep', 'shard'), split_axis=0, concat_axis=0, til...  6.28 us
  transfers between devices with their start and end apart: 1, of which 1 were waited for; matrix products, arithmetic and copies ran while one was open for 6% of the time, Pallas kernels for 0%

profile of v1, /device:TPU:1, one launch (start us, length us, event | category | flops | bytes accessed | tf_op | source)
XLA Modules:
  0.0 252.1 jit_solution(16357699340330017912)
XLA Ops:
  0.6 1.2 slice.21
  3.5 0.9 copy.40
  8.1 1.1 copy-done.2
  9.2 1.0 copy-done.3
  10.1 1.0 copy-done.4
  11.1 78.8 %shard_map.195 = (bf16[384,768]{1,0:T(8,128)(2,1)S(1)}, bf16[384,1152]{1,0:T(8,128)(2,1)S(1)}, bf16[6,384,384]{2,1,0:T(8,128)(2,1)}, bf16[384,384]{1,0:T(8,128)(...) custom-call(bf16[192,768]{1,0:T(8,128)(2,1)S(1)} %copy-done.3, ...), custom_call_target="tpu_custom_call" | custom-call | flops 30000001024 | bytes 100000000 | tf_op jit(solution)/shard_map/pallas_call | solution.py:339
  89.9 0.9 copy-done.7
  91.7 1.9 copy-done.6
  93.6 12.8 %shard_map.196 = (bf16[1024,1536]{1,0:T(8,128)(2,1)}, bf16[1024,1536]{1,0:T(8,128)(2,1)}, bf16[1024,768]{1,0:T(8,128)(2,1)}, bf16[1024,768]{1,0:T(8,128)(2,1)S(1)}, bf16[1024,768]{1,0:T(8,128)(2,1)S(1)}) custom-call(bf16[1024,768]{1,0:T(8,128)(2,1)S(1)} %bitcast.26, bf16[1024,768]{1,0:T(8,128)(2,1)S(1)} %bitcast.30, bf16[768,1536]{1,0:T(8,128)(2,1)S(1)} %bitcast.27, ...), custom_call_target="tpu_custom_call" | custom-call | flops 9663676416 | bytes 20000000 | tf_op jit(solution)/shard_map/pallas_call | solution.py:409
  106.4 1.2 copy-done.5
  107.6 6.3 %all-to-all-start = ((bf16[128,8,768]{2,1,0:T(8,128)(2,1)}), bf16[128,8,768]{2,1,0:T(8,128)(2,1)}, u32[]{:S(2)}, u32[]{:S(2)}) async-start(bf16[128,8,768]{2,1,0:T(8,128)(2,1)} %bitcast.6), calls=%async_computation | async-start | bytes 3145728 | tf_op jit(solution)/shard_map/all_to_all | solution.py:915
  114.0 0.8 copy.43
  115.4 1.8 broadcast_in_dim.22
  117.2 2.0 copy.44.dispatch_ref
  119.2 6.3 %convolution_bitcast_fusion.1 = f32[1,768,1536]{2,1,0:T(8,128)} fusion(bf16[1024,1536]{1,0:T(8,128)(2,1)} %get-tuple-element.51, bf16[128,8,768]{2,1,0:T(8,128)(2,1)S(1)} %get-tuple-element.32), kind=kOutput, calls=%fused_computation.1 | convolution fusion | flops 2415919104 | bytes 9437184 | tf_op jit(solution)/shard_map/dot_general | solution.py:75
  125.5 4.3 %convolution_bitcast_fusion = f32[1,1536,768]{2,1,0:T(8,128)} fusion(bf16[1024,1536]{1,0:T(8,128)(2,1)S(1)} %copy-done.18, bf16[1024,768]{1,0:T(8,128)(2,1)S(1)} %get-tuple-element.53), kind=kOutput, calls=%fused_computation | convolution fusion | flops 2415919104 | bytes 9437184 | tf_op jit(solution)/shard_map/dot_general | solution.py:75
  129.8 8.3 %all-to-all-done = bf16[128,8,768]{2,1,0:T(8,128)(2,1)} async-done(((bf16[128,8,768]{2,1,0:T(8,128)(2,1)}), bf16[128,8,768]{2,1,0:T(8,128)(2,1)}, u32[]{:S(2)}, u32[]{:S(2)}) %all-to-all-start) | async-done | bytes 1572896 | tf_op jit(solution)/shard_map/all_to_all | solution.py:915
  138.1 103.9 %shard_map.197 = (bf16[192,768]{1,0:T(8,128)(2,1)}, f32[192,768]{1,0:T(8,128)}, bf16[384,2304]{1,0:T(8,128)(2,1)}, bf16[384,768]{1,0:T(8,128)(2,1)}, f32[384,128]{1,0:T(8,128)}, /*index=5*/f32[32,128]{1,0:T(8,128)}) custom-call(bf16[1024,768]{1,0:T(8,128)(2,1)} %bitcast.7.sent_ref, bf16[128,8,768]{2,1,0:T(8,128)(2,1)} %bitcast.29, ...), custom_call_target="tpu_custom_call" | custom-call | flops 60000002048 | bytes 200000000 | tf_op jit(solution)/shard_map/pallas_call | solution.py:848
  242.0 1.4 slice_bitcast_fusion
  243.4 1.3 slice.25
  244.7 1.7 copy.45
  246.4 2.2 convert_element_type.38
  248.6 2.0 convert_element_type.37
  251.3 0.8 copy.49
  (52 shorter events, 7.6 us)
Async XLA Ops:
  8.1 1.1 copy-start.2
  9.1 1.0 copy-start.3
  10.1 1.0 copy-start.4
  11.1 80.6 %copy-start = (bf16[1,768,1536]{2,1,0:T(8,128)(2,1)S(1)}, bf16[1,768,1536]{2,1,0:T(8,128)(2,1)}, u32[]{:S(2)}) copy-start(bf16[1,768,1536]{2,1,0:T(8,128)(2,1)} %param.21) | copy-start | bytes 7077892
  11.1 80.6 %copy-start.1 = (bf16[1,1536,768]{2,1,0:T(8,128)(2,1)S(1)}, bf16[1,1536,768]{2,1,0:T(8,128)(2,1)}, u32[]{:S(2)}) copy-start(bf16[1,1536,768]{2,1,0:T(8,128)(2,1)} %param.22) | copy-start | bytes 7077892
  89.9 0.9 copy-start.7
  90.8 0.8 copy-start.8
  91.6 14.7 %copy-start.9 = (f32[192,768]{1,0:T(8,128)}, f32[192,768]{1,0:T(8,128)S(1)}, u32[]{:S(2)}) copy-start(f32[192,768]{1,0:T(8,128)S(1)} %get-tuple-element.42.hidden_ref) | copy-start | bytes 1769476
  91.6 14.7 %copy-start.10 = (bf16[384,384]{1,0:T(8,128)(2,1)}, bf16[384,384]{1,0:T(8,128)(2,1)S(1)}, u32[]{:S(2)}) copy-start(bf16[384,384]{1,0:T(8,128)(2,1)S(1)} %get-tuple-element.39.mixed_ref) | copy-start | bytes 884740
  91.6 14.7 %copy-start.11 = (bf16[192,768]{1,0:T(8,128)(2,1)}, bf16[192,768]{1,0:T(8,128)(2,1)S(1)}, u32[]{:S(2)}) copy-start(bf16[192,768]{1,0:T(8,128)(2,1)S(1)} %get-tuple-element.43.n2_ref) | copy-start | bytes 884740
  91.6 14.7 %copy-start.12 = (bf16[2,416,128]{2,1,0:T(8,128)(2,1)}, bf16[2,416,128]{2,1,0:T(8,128)(2,1)S(1)}, u32[]{:S(2)}) copy-start(bf16[2,416,128]{2,1,0:T(8,128)(2,1)S(1)} %get-tuple-element.41.small_all) | copy-start | bytes 638980
  91.6 14.7 %copy-start.13 = (f32[192,128]{1,0:T(8,128)}, f32[192,128]{1,0:T(8,128)S(1)}, u32[]{:S(2)}) copy-start(f32[192,128]{1,0:T(8,128)S(1)} %get-tuple-element.44.router_ref) | copy-start | bytes 294916
  91.7 1.9 copy-start.6
  106.4 1.2 copy-start.5
  107.6 6.3 %copy-start.17 = (s32[384]{0:T(512)S(1)}, s32[384]{0:T(512)}, u32[]{:S(2)}) copy-start(s32[384]{0:T(512)} %param.18) | copy-start | bytes 4612
  107.6 30.5 %all-to-all-start = ((bf16[128,8,768]{2,1,0:T(8,128)(2,1)}), bf16[128,8,768]{2,1,0:T(8,128)(2,1)}, u32[]{:S(2)}, u32[]{:S(2)}) async-start(bf16[128,8,768]{2,1,0:T(8,128)(2,1)} %bitcast.6), calls=%async_computation | async-start | bytes 3145728 | tf_op jit(solution)/shard_map/all_to_all | solution.py:915
  119.2 6.3 %copy-start.18 = (bf16[1024,1536]{1,0:T(8,128)(2,1)S(1)}, bf16[1024,1536]{1,0:T(8,128)(2,1)}, u32[]{:S(2)}) copy-start(bf16[1024,1536]{1,0:T(8,128)(2,1)} %get-tuple-element.52) | copy-start | bytes 9437188
  242.0 6.5 %copy-start.14 = (bf16[384,2304]{1,0:T(8,128)(2,1)S(1)}, bf16[384,2304]{1,0:T(8,128)(2,1)}, u32[]{:S(2)}) copy-start(bf16[384,2304]{1,0:T(8,128)(2,1)} %get-tuple-element.48) | copy-start | bytes 5308420
  248.6 2.0 copy-start.16
  248.6 2.7 %copy-start.15 = (f32[192,768]{1,0:T(8,128)S(1)}, f32[192,768]{1,0:T(8,128)}, u32[]{:S(2)}) copy-start(f32[192,768]{1,0:T(8,128)} %get-tuple-element.107) | copy-start | bytes 1769476

commit v2 on v0

--- a/solution.py
+++ b/solution.py
@@ -131,6 +131,16 @@
     spread = jnp.where(lane == slot, high.astype(F32), 0.0)
     spread = spread + jnp.where(lane == slot + capacity, low.astype(F32), 0.0)
     return matmul(carrier, spread.astype(BF16))
+
+
+def bucket_mask(bucket_ref, buckets, distance):
+    row = bucket_ref[...]
+    levels = iota((buckets, row.shape[1]), 0)
+    low = jnp.sum((row < levels).astype(F32), axis=1, keepdims=True)
+    high = jnp.sum((row <= levels).astype(F32), axis=1, keepdims=True)
+    distance = distance.astype(F32)
+    inside = (distance >= low) & (distance < high)
+    return inside.astype(F32).astype(BF16)
 
 
 def front_kernel(
@@ -228,8 +238,9 @@
     small_copy.wait()
 
     table = jnp.concatenate([small_all[0, half + 16 :, :], small_all[1, half + 16 :, :]], axis=0)
-    levels = iota((buckets, 2 * seq), 0)
-    one_hot = (levels == bucket_ref[...]).astype(F32).astype(BF16)
+    column = iota((buckets, 2 * seq), 1)
+    distance = jnp.where(column == 0, 0, 2 * seq - column)
+    one_hot = bucket_mask(bucket_ref, buckets, distance)
     bias_rows[...] = t_matmul(table, one_hot)
     gain_one = gain_row(small_all, half, 0)
     gain_two = gain_row(small_all, half, half // 128)
@@ -616,8 +627,7 @@
         grad = t_matmul(n1_ref[...], dqkv[:, block * 128 : (block + 1) * 128]).astype(BF16)
         for side in range(2):
             store(side, block * half, grad[side * half : (side + 1) * half])
-    levels = iota((buckets, 2 * seq), 0)
-    one_hot = (levels == bucket_ref[...]).astype(F32).astype(BF16)
+    one_hot = bucket_mask(bucket_ref, buckets, seq - 1 - iota((buckets, 2 * seq), 1))
     high, low = two_parts(sums[...])
     g_table = (matmul_t(one_hot, high) + matmul_t(one_hot, low)).astype(BF16)
     for side in range(2):
@@ -644,6 +654,22 @@
 
     first, second = pl.ds(0, cut), pl.ds(cut, chunk_rows - cut)
     chip_copy = send_to(comm.at[:, 1 - core], chip_in, core_peer)
+    finish([chip_copy])
+
+    def add_chip(i, carry):
+        total = comm[i, core].astype(F32) + chip_in[i].astype(F32)
+        chip[i // (xs * zs), lax.rem(i // zs, xs), lax.rem(i, zs)] = total.astype(BF16)
+        return carry
+
+    lax.fori_loop(0, ys * xs * zs, add_chip, 0)
+    copies = [
+        send_to(chip.at[:, at, :, first], row_in.at[i], to)
+        for i, (at, to) in enumerate(zip(xp, x_peers))
+    ]
+    copies += [
+        send_to(chip.at[at, :, :, second], column_in.at[i], to)
+        for i, (at, to) in enumerate(zip(yp, y_peers))
+    ]
 
     own_block.wait()
     wait_blocks(returned, devices, all_sems.at[0], all_sems.at[1])
@@ -661,22 +687,6 @@
         for part in two_parts(weights):
             layer = layer + matmul(part, block)
     layer_ref[...] = layer.astype(BF16)
-    finish([chip_copy])
-
-    def add_chip(i, carry):
-        total = comm[i, core].astype(F32) + chip_in[i].astype(F32)
-        chip[i // (xs * zs), lax.rem(i // zs, xs), lax.rem(i, zs)] = total.astype(BF16)
-        return carry
-
-    lax.fori_loop(0, ys * xs * zs, add_chip, 0)
-    copies = [
-        send_to(chip.at[:, at, :, first], row_in.at[i], to)
-        for i, (at, to) in enumerate(zip(xp, x_peers))
-    ]
-    copies += [
-        send_to(chip.at[at, :, :, second], column_in.at[i], to)
-        for i, (at, to) in enumerate(zip(yp, y_peers))
-    ]
     finish(copies)
 
     def add_row(i, carry):
@@ -765,7 +775,8 @@
             gqkv_ref[:, at : at + 128] = load(side, block * half, half)
     for block in range(2 * blocks):
         gout_w_ref[:, block * 128 : (block + 1) * 128] = load(2, block * half, half)
-    grouter_ref[...] = sum(load(side, tile_rows, half).astype(F32) for side in range(2))
+    g_router = sum(load(side, tile_rows, half).astype(F32) for side in range(2))
+    grouter_ref[...] = g_router.T[:experts]
     gsmall_ref[...] = sum(
         load(side, tile_rows + half, 16 + buckets // 2).astype(F32) for side in range(2)
     )
@@ -787,7 +798,7 @@
         ((rows, width), F32),
         ((half, 3 * width), BF16),
         ((half, width), BF16),
-        ((half, 128), F32),
+        ((experts, half), F32),
         ((16 + buckets // 2, 128), F32),
     ]
     return pl.pallas_call(
@@ -877,12 +888,9 @@
             jnp.pad(rel_bias, ((0, 0), (0, 128 - heads))),
         ]
     )
-    nothing = jnp.full((seq,), -1, jnp.int32)
-    back_order = buckets[::-1]
-    bucket_front = jnp.concatenate([buckets[:1], nothing, back_order[:-1]]).reshape(1, 2 * seq)
-    bucket_back = jnp.concatenate([back_order, nothing]).reshape(1, 2 * seq)
+    bucket_row = buckets.reshape(1, seq)
     *kept, arrived, grad_rows = front(
-        sizes, dims, tokens, small, w_qkv, w_out, bucket_front, dispatch, cotangent
+        sizes, dims, tokens, small, w_qkv, w_out, bucket_row, dispatch, cotangent
     )
     arrived, grad_rows = (block.reshape(2 * slots, width) for block in (arrived, grad_rows))
 
@@ -896,7 +904,7 @@
     grad_in_expert = t_matmul(arrived, grad_pre)
 
     layer_out, grad_tokens, g_qkv, g_out, g_router, g_small = back(
-        sizes, dims, sent, result, dispatch_two, cotangent, tokens, kept, w_out, bucket_back
+        sizes, dims, sent, result, dispatch_two, cotangent, tokens, kept, w_out, bucket_row
     )
 
     return (
@@ -907,7 +915,7 @@
         g_out.astype(F32),
         g_small[16:, :heads],
         g_small[blocks : 2 * blocks].reshape(half),
-        g_router[:, :experts],
+        g_router.T,
         grad_in_expert[None],
         grad_back_expert[None],
     )

time: 247 us -> 243 us (0.984)
  local copies, waits for them, and re-layouts: 23.3 us -> 20.1 us
where the time goes in v2:
time: 243 us; the launch traced here: 242 us
  Pallas kernels  188 us (77%)
  local copies, waits for them, and re-layouts  20.1 us (8%)
  matrix products  10.8 us (4%)
  waiting for transfers between devices  8.93 us (4%)
  starting transfers between devices  7.33 us (3%)
  other arithmetic  6.44 us (3%)
    pallas_call x1, Pallas kernels, back(): pl.pallas_call(functools.partial(back_kernel, sizes, dims, both, cut), ou...  99.8 us
    pallas_call x1, Pallas kernels, front(): pl.pallas_call(functools.partial(front_kernel, sizes, dims), out_shape=[j...  75.2 us
    pallas_call x1, Pallas kernels, expert(): pl.pallas_call(functools.partial(expert_kernel, capacity), grid=(count //...  12.8 us
    unnamed x45, local copies, waits for them, and re-layouts  11.7 us
    dot_general x3, matrix products, dot(): lax.dot_general(a, b, (contract, ((), ())), preferred_element_type=F32)  10.8 us
    all_to_all x1, waiting for transfers between devices, swap_all(): lax.all_to_all(blocks, ('rep', 'shard'), split_axis=0, concat_axis=0, til...  8.93 us
    all_to_all x1, starting transfers between devices, swap_all(): lax.all_to_all(blocks, ('rep', 'shard'), split_axis=0, concat_axis=0, til...  7.33 us
  transfers between devices with their start and end apart: 1, of which 1 were waited for; matrix products, arithmetic and copies ran while one was open for 6% of the time, Pallas kernels for 0%

profile of v2, /device:TPU:1, one launch (start us, length us, event | category | flops | bytes accessed | tf_op | source)
XLA Modules:
  0.0 242.2 jit_solution(18184236563025106458)
XLA Ops:
  1.3 0.9 copy.37
  2.2 0.8 copy.38
  5.9 1.1 copy-done.3
  7.0 1.0 copy-done.4
  8.0 1.0 copy-done.5
  8.9 75.2 %shard_map.195 = (bf16[384,768]{1,0:T(8,128)(2,1)S(1)}, bf16[384,1152]{1,0:T(8,128)(2,1)S(1)}, bf16[6,384,384]{2,1,0:T(8,128)(2,1)}, bf16[384,384]{1,0:T(8,128)(...) custom-call(bf16[192,768]{1,0:T(8,128)(2,1)S(1)} %copy-done.4, ...), custom_call_target="tpu_custom_call" | custom-call | flops 30000001024 | bytes 100000000 | tf_op jit(solution)/shard_map/pallas_call | solution.py:350
  84.2 0.9 copy-done.8
  85.1 0.8 copy-done.9
  85.9 1.9 copy-done.7
  87.8 12.8 %shard_map.196 = (bf16[1024,1536]{1,0:T(8,128)(2,1)}, bf16[1024,1536]{1,0:T(8,128)(2,1)}, bf16[1024,768]{1,0:T(8,128)(2,1)}, bf16[1024,768]{1,0:T(8,128)(2,1)S(1)}, bf16[1024,768]{1,0:T(8,128)(2,1)S(1)}) custom-call(bf16[1024,768]{1,0:T(8,128)(2,1)S(1)} %bitcast.25, bf16[1024,768]{1,0:T(8,128)(2,1)S(1)} %bitcast.29, bf16[768,1536]{1,0:T(8,128)(2,1)S(1)} %bitcast.26, ...), custom_call_target="tpu_custom_call" | custom-call | flops 9663676416 | bytes 20000000 | tf_op jit(solution)/shard_map/pallas_call | solution.py:420
  100.6 1.2 copy-done.6
  101.8 7.3 %all-to-all-start = ((bf16[128,8,768]{2,1,0:T(8,128)(2,1)}), bf16[128,8,768]{2,1,0:T(8,128)(2,1)}, u32[]{:S(2)}, u32[]{:S(2)}) async-start(bf16[128,8,768]{2,1,0:T(8,128)(2,1)} %bitcast.6), calls=%async_computation | async-start | bytes 3145728 | tf_op jit(solution)/shard_map/all_to_all | solution.py:880
  109.2 0.9 copy.40
  110.0 1.8 broadcast_in_dim.18
  111.8 2.0 copy.41.dispatch_ref
  113.8 6.3 %convolution_bitcast_fusion.1 = f32[1,768,1536]{2,1,0:T(8,128)} fusion(bf16[1024,1536]{1,0:T(8,128)(2,1)} %get-tuple-element.51, bf16[128,8,768]{2,1,0:T(8,128)(2,1)S(1)} %get-tuple-element.32), kind=kOutput, calls=%fused_computation.1 | convolution fusion | flops 2415919104 | bytes 9437184 | tf_op jit(solution)/shard_map/dot_general | solution.py:75
  120.1 4.3 %convolution_bitcast_fusion = f32[1,1536,768]{2,1,0:T(8,128)} fusion(bf16[1024,1536]{1,0:T(8,128)(2,1)S(1)} %copy-done.19, bf16[1024,768]{1,0:T(8,128)(2,1)S(1)} %get-tuple-element.53), kind=kOutput, calls=%fused_computation | convolution fusion | flops 2415919104 | bytes 9437184 | tf_op jit(solution)/shard_map/dot_general | solution.py:75
  124.4 8.9 %all-to-all-done = bf16[128,8,768]{2,1,0:T(8,128)(2,1)} async-done(((bf16[128,8,768]{2,1,0:T(8,128)(2,1)}), bf16[128,8,768]{2,1,0:T(8,128)(2,1)}, u32[]{:S(2)}, u32[]{:S(2)}) %all-to-all-start) | async-done | bytes 1572896 | tf_op jit(solution)/shard_map/all_to_all | solution.py:880
  133.4 99.8 %shard_map.197 = (bf16[192,768]{1,0:T(8,128)(2,1)}, f32[192,768]{1,0:T(8,128)}, bf16[384,2304]{1,0:T(8,128)(2,1)}, bf16[384,768]{1,0:T(8,128)(2,1)}, f32[64,384]{1,0:T(8,128)}, /*index=5*/f32[32,128]{1,0:T(8,128)}) custom-call(bf16[1024,768]{1,0:T(8,128)(2,1)} %bitcast.7.sent_ref, bf16[128,8,768]{2,1,0:T(8,128)(2,1)} %bitcast.28, ...), custom_call_target="tpu_custom_call" | custom-call | flops 60000002048 | bytes 200000000 | tf_op jit(solution)/shard_map/pallas_call | solution.py:804
  233.2 1.4 slice_bitcast_fusion
  234.6 1.3 slice.10
  235.9 2.2 convert_element_type.38
  238.0 2.0 convert_element_type.37
  240.8 0.8 copy.46
  (45 shorter events, 4.9 us)
Async XLA Ops:
  1.3 82.8 %copy-start = (s32[1,384]{1,0:T(1,128)}, s32[1,384]{1,0:T(1,128)S(1)}, u32[]{:S(2)}) copy-start(s32[1,384]{1,0:T(1,128)S(1)} %reshape.67.bucket_ref) | copy-start | bytes 4612
  5.9 1.1 copy-start.3
  7.0 1.0 copy-start.4
  7.9 1.0 copy-start.5
  8.9 77.0 %copy-start.1 = (bf16[1,768,1536]{2,1,0:T(8,128)(2,1)S(1)}, bf16[1,768,1536]{2,1,0:T(8,128)(2,1)}, u32[]{:S(2)}) copy-start(bf16[1,768,1536]{2,1,0:T(8,128)(2,1)} %param.21) | copy-start | bytes 7077892
  8.9 77.0 %copy-start.2 = (bf16[1,1536,768]{2,1,0:T(8,128)(2,1)S(1)}, bf16[1,1536,768]{2,1,0:T(8,128)(2,1)}, u32[]{:S(2)}) copy-start(bf16[1,1536,768]{2,1,0:T(8,128)(2,1)} %param.22) | copy-start | bytes 7077892
  84.1 0.9 copy-start.8
  85.1 0.8 copy-start.9
  85.9 14.7 %copy-start.10 = (f32[192,768]{1,0:T(8,128)}, f32[192,768]{1,0:T(8,128)S(1)}, u32[]{:S(2)}) copy-start(f32[192,768]{1,0:T(8,128)S(1)} %get-tuple-element.42.hidden_ref) | copy-start | bytes 1769476
  85.9 14.7 %copy-start.11 = (bf16[384,384]{1,0:T(8,128)(2,1)}, bf16[384,384]{1,0:T(8,128)(2,1)S(1)}, u32[]{:S(2)}) copy-start(bf16[384,384]{1,0:T(8,128)(2,1)S(1)} %get-tuple-element.39.mixed_ref) | copy-start | bytes 884740
  85.9 14.7 %copy-start.12 = (bf16[192,768]{1,0:T(8,128)(2,1)}, bf16[192,768]{1,0:T(8,128)(2,1)S(1)}, u32[]{:S(2)}) copy-start(bf16[192,768]{1,0:T(8,128)(2,1)S(1)} %get-tuple-element.43.n2_ref) | copy-start | bytes 884740
  85.9 14.7 %copy-start.13 = (bf16[2,416,128]{2,1,0:T(8,128)(2,1)}, bf16[2,416,128]{2,1,0:T(8,128)(2,1)S(1)}, u32[]{:S(2)}) copy-start(bf16[2,416,128]{2,1,0:T(8,128)(2,1)S(1)} %get-tuple-element.41.small_all) | copy-start | bytes 638980
  85.9 14.7 %copy-start.14 = (f32[192,128]{1,0:T(8,128)}, f32[192,128]{1,0:T(8,128)S(1)}, u32[]{:S(2)}) copy-start(f32[192,128]{1,0:T(8,128)S(1)} %get-tuple-element.44.router_ref) | copy-start | bytes 294916
  85.9 1.9 copy-start.7
  100.6 1.2 copy-start.6
  101.8 31.5 %all-to-all-start = ((bf16[128,8,768]{2,1,0:T(8,128)(2,1)}), bf16[128,8,768]{2,1,0:T(8,128)(2,1)}, u32[]{:S(2)}, u32[]{:S(2)}) async-start(bf16[128,8,768]{2,1,0:T(8,128)(2,1)} %bitcast.6), calls=%async_computation | async-start | bytes 3145728 | tf_op jit(solution)/shard_map/all_to_all | solution.py:880
  113.8 6.3 %copy-start.19 = (bf16[1024,1536]{1,0:T(8,128)(2,1)S(1)}, bf16[1024,1536]{1,0:T(8,128)(2,1)}, u32[]{:S(2)}) copy-start(bf16[1024,1536]{1,0:T(8,128)(2,1)} %get-tuple-element.52) | copy-start | bytes 9437188
  233.2 4.9 %copy-start.15 = (bf16[384,2304]{1,0:T(8,128)(2,1)S(1)}, bf16[384,2304]{1,0:T(8,128)(2,1)}, u32[]{:S(2)}) copy-start(bf16[384,2304]{1,0:T(8,128)(2,1)} %get-tuple-element.48) | copy-start | bytes 5308420
  238.0 2.0 copy-start.17
  238.0 2.7 %copy-start.16 = (f32[192,768]{1,0:T(8,128)S(1)}, f32[192,768]{1,0:T(8,128)}, u32[]{:S(2)}) copy-start(f32[192,768]{1,0:T(8,128)} %get-tuple-element.67) | copy-start | bytes 1769476
  240.1 1.5 copy-start.18

commit v3 on v2

--- a/solution.py
+++ b/solution.py
@@ -34,7 +34,7 @@
     me = 2 * lax.axis_index("rep") + lax.axis_index("shard")
 
     def start(step, carry):
-        to = lax.rem(me + step, count)
+        to = lax.rem(me + 37 * step, count)
         pltpu.make_async_remote_copy(
             source_of(to),
             target.at[me],
@@ -557,9 +557,6 @@
     )
     att_all[mine] = d_hidden.astype(BF16)
     shared = send_to(att_all.at[mine], att_all.at[mine], peer)
-    send_blocks(lambda to: result_ref.at[to], returned, devices, all_sems.at[0], all_sems.at[1])
-    own_block = pltpu.make_async_copy(result_ref.at[me], returned.at[me], all_sems.at[2])
-    own_block.start()
     gtok_ref[...] = d_hidden
     g_gain_two = jnp.sum(d_n2 * unit, axis=0, keepdims=True)
     g_router = t_matmul(n2_ref[...], d_logits)
@@ -580,6 +577,9 @@
     for side in range(2):
         store(side, tile_rows, g_router[side * half : (side + 1) * half].astype(BF16))
     shared.wait()
+    send_blocks(lambda to: result_ref.at[to], returned, devices, all_sems.at[0], all_sems.at[1])
+    own_block = pltpu.make_async_copy(result_ref.at[me], returned.at[me], all_sems.at[2])
+    own_block.start()
 
     d_att = [att_all[0], att_all[1]]
     for block in range(2 * blocks):

time: 243 us -> 234 us (0.963)
  Pallas kernels: 188 us -> 181 us
    pallas_call x1, Pallas kernels: 99.8 us -> 94.4 us  [back(): pl.pallas_call(functools.partial(back_kernel, sizes, dims, both, cut), ou...]
  transfers between devices with their start and end apart: 1 -> 1, of which waited for: 1 -> 1; matrix products, arithmetic and copies ran while one was open for 6% -> 7% of each run, Pallas kernels for 0% -> 0%
where the time goes in v3:
time: 234 us; the launch traced here: 233 us
  Pallas kernels  181 us (77%)
  local copies, waits for them, and re-layouts  20.1 us (9%)
  matrix products  10.8 us (5%)
  waiting for transfers between devices  8.93 us (4%)
  other arithmetic  6.44 us (3%)
  starting transfers between devices  5.49 us (2%)
    pallas_call x1, Pallas kernels, back(): pl.pallas_call(functools.partial(back_kernel, sizes, dims, both, cut), ou...  94.4 us
    pallas_call x1, Pallas kernels, front(): pl.pallas_call(functools.partial(front_kernel, sizes, dims), out_shape=[j...  73.5 us
    pallas_call x1, Pallas kernels, expert(): pl.pallas_call(functools.partial(expert_kernel, capacity), grid=(count //...  12.8 us
    unnamed x45, local copies, waits for them, and re-layouts  11.7 us
    dot_general x3, matrix products, dot(): lax.dot_general(a, b, (contract, ((), ())), preferred_element_type=F32)  10.8 us
    all_to_all x1, waiting for transfers between devices, swap_all(): lax.all_to_all(blocks, ('rep', 'shard'), split_axis=0, concat_axis=0, til...  8.93 us
    all_to_all x1, starting transfers between devices, swap_all(): lax.all_to_all(blocks, ('rep', 'shard'), split_axis=0, concat_axis=0, til...  5.49 us
  transfers between devices with their start and end apart: 1, of which 1 were waited for; matrix products, arithmetic and copies ran while one was open for 7% of the time, Pallas kernels for 0%

profile of v3, /device:TPU:1, one launch (start us, length us, event | category | flops | bytes accessed | tf_op | source)
XLA Modules:
  0.0 233.4 jit_solution(17151634835353359307)
XLA Ops:
  1.3 0.9 copy.37
  2.2 0.8 copy.38
  5.9 1.1 copy-done.3
  7.0 1.0 copy-done.4
  8.0 1.0 copy-done.5
  8.9 73.5 %shard_map.195 = (bf16[384,768]{1,0:T(8,128)(2,1)S(1)}, bf16[384,1152]{1,0:T(8,128)(2,1)S(1)}, bf16[6,384,384]{2,1,0:T(8,128)(2,1)}, bf16[384,384]{1,0:T(8,128)(...) custom-call(bf16[192,768]{1,0:T(8,128)(2,1)S(1)} %copy-done.4, ...), custom_call_target="tpu_custom_call" | custom-call | flops 30000001024 | bytes 100000000 | tf_op jit(solution)/shard_map/pallas_call | solution.py:350
  82.5 0.9 copy-done.8
  83.4 0.8 copy-done.9
  84.3 1.9 copy-done.7
  86.2 12.8 %shard_map.196 = (bf16[1024,1536]{1,0:T(8,128)(2,1)}, bf16[1024,1536]{1,0:T(8,128)(2,1)}, bf16[1024,768]{1,0:T(8,128)(2,1)}, bf16[1024,768]{1,0:T(8,128)(2,1)S(1)}, bf16[1024,768]{1,0:T(8,128)(2,1)S(1)}) custom-call(bf16[1024,768]{1,0:T(8,128)(2,1)S(1)} %bitcast.25, bf16[1024,768]{1,0:T(8,128)(2,1)S(1)} %bitcast.29, bf16[768,1536]{1,0:T(8,128)(2,1)S(1)} %bitcast.26, ...), custom_call_target="tpu_custom_call" | custom-call | flops 9663676416 | bytes 20000000 | tf_op jit(solution)/shard_map/pallas_call | solution.py:420
  99.0 1.2 copy-done.6
  100.2 5.5 %all-to-all-start = ((bf16[128,8,768]{2,1,0:T(8,128)(2,1)}), bf16[128,8,768]{2,1,0:T(8,128)(2,1)}, u32[]{:S(2)}, u32[]{:S(2)}) async-start(bf16[128,8,768]{2,1,0:T(8,128)(2,1)} %bitcast.6), calls=%async_computation | async-start | bytes 3145728 | tf_op jit(solution)/shard_map/all_to_all | solution.py:880
  105.7 0.9 copy.40
  106.5 1.8 broadcast_in_dim.18
  108.3 2.0 copy.41.dispatch_ref
  110.3 6.3 %convolution_bitcast_fusion.1 = f32[1,768,1536]{2,1,0:T(8,128)} fusion(bf16[1024,1536]{1,0:T(8,128)(2,1)} %get-tuple-element.51, bf16[128,8,768]{2,1,0:T(8,128)(2,1)S(1)} %get-tuple-element.32), kind=kOutput, calls=%fused_computation.1 | convolution fusion | flops 2415919104 | bytes 9437184 | tf_op jit(solution)/shard_map/dot_general | solution.py:75
  116.6 4.3 %convolution_bitcast_fusion = f32[1,1536,768]{2,1,0:T(8,128)} fusion(bf16[1024,1536]{1,0:T(8,128)(2,1)S(1)} %copy-done.19, bf16[1024,768]{1,0:T(8,128)(2,1)S(1)} %get-tuple-element.53), kind=kOutput, calls=%fused_computation | convolution fusion | flops 2415919104 | bytes 9437184 | tf_op jit(solution)/shard_map/dot_general | solution.py:75
  120.9 8.9 %all-to-all-done = bf16[128,8,768]{2,1,0:T(8,128)(2,1)} async-done(((bf16[128,8,768]{2,1,0:T(8,128)(2,1)}), bf16[128,8,768]{2,1,0:T(8,128)(2,1)}, u32[]{:S(2)}, u32[]{:S(2)}) %all-to-all-start) | async-done | bytes 1572896 | tf_op jit(solution)/shard_map/all_to_all | solution.py:880
  129.9 94.4 %shard_map.197 = (bf16[192,768]{1,0:T(8,128)(2,1)}, f32[192,768]{1,0:T(8,128)}, bf16[384,2304]{1,0:T(8,128)(2,1)}, bf16[384,768]{1,0:T(8,128)(2,1)}, f32[64,384]{1,0:T(8,128)}, /*index=5*/f32[32,128]{1,0:T(8,128)}) custom-call(bf16[1024,768]{1,0:T(8,128)(2,1)} %bitcast.7.sent_ref, bf16[128,8,768]{2,1,0:T(8,128)(2,1)} %bitcast.28, ...), custom_call_target="tpu_custom_call" | custom-call | flops 60000002048 | bytes 200000000 | tf_op jit(solution)/shard_map/pallas_call | solution.py:804
  224.3 1.4 slice_bitcast_fusion
  225.7 1.3 slice.10
  227.0 2.2 convert_element_type.38
  229.2 2.0 convert_element_type.37
  231.9 0.8 copy.46
  (45 shorter events, 4.9 us)
Async XLA Ops:
  1.3 81.1 %copy-start = (s32[1,384]{1,0:T(1,128)}, s32[1,384]{1,0:T(1,128)S(1)}, u32[]{:S(2)}) copy-start(s32[1,384]{1,0:T(1,128)S(1)} %reshape.67.bucket_ref) | copy-start | bytes 4612
  5.9 1.1 copy-start.3
  7.0 1.0 copy-start.4
  7.9 1.0 copy-start.5
  8.9 75.3 %copy-start.1 = (bf16[1,768,1536]{2,1,0:T(8,128)(2,1)S(1)}, bf16[1,768,1536]{2,1,0:T(8,128)(2,1)}, u32[]{:S(2)}) copy-start(bf16[1,768,1536]{2,1,0:T(8,128)(2,1)} %param.21) | copy-start | bytes 7077892
  8.9 75.3 %copy-start.2 = (bf16[1,1536,768]{2,1,0:T(8,128)(2,1)S(1)}, bf16[1,1536,768]{2,1,0:T(8,128)(2,1)}, u32[]{:S(2)}) copy-start(bf16[1,1536,768]{2,1,0:T(8,128)(2,1)} %param.22) | copy-start | bytes 7077892
  82.5 0.9 copy-start.8
  83.4 0.8 copy-start.9
  84.2 14.7 %copy-start.10 = (f32[192,768]{1,0:T(8,128)}, f32[192,768]{1,0:T(8,128)S(1)}, u32[]{:S(2)}) copy-start(f32[192,768]{1,0:T(8,128)S(1)} %get-tuple-element.42.hidden_ref) | copy-start | bytes 1769476
  84.2 14.7 %copy-start.11 = (bf16[384,384]{1,0:T(8,128)(2,1)}, bf16[384,384]{1,0:T(8,128)(2,1)S(1)}, u32[]{:S(2)}) copy-start(bf16[384,384]{1,0:T(8,128)(2,1)S(1)} %get-tuple-element.39.mixed_ref) | copy-start | bytes 884740
  84.2 14.7 %copy-start.12 = (bf16[192,768]{1,0:T(8,128)(2,1)}, bf16[192,768]{1,0:T(8,128)(2,1)S(1)}, u32[]{:S(2)}) copy-start(bf16[192,768]{1,0:T(8,128)(2,1)S(1)} %get-tuple-element.43.n2_ref) | copy-start | bytes 884740
  84.2 14.7 %copy-start.13 = (bf16[2,416,128]{2,1,0:T(8,128)(2,1)}, bf16[2,416,128]{2,1,0:T(8,128)(2,1)S(1)}, u32[]{:S(2)}) copy-start(bf16[2,416,128]{2,1,0:T(8,128)(2,1)S(1)} %get-tuple-element.41.small_all) | copy-start | bytes 638980
  84.2 14.7 %copy-start.14 = (f32[192,128]{1,0:T(8,128)}, f32[192,128]{1,0:T(8,128)S(1)}, u32[]{:S(2)}) copy-start(f32[192,128]{1,0:T(8,128)S(1)} %get-tuple-element.44.router_ref) | copy-start | bytes 294916
  84.2 1.9 copy-start.7
  99.0 1.2 copy-start.6
  100.2 29.7 %all-to-all-start = ((bf16[128,8,768]{2,1,0:T(8,128)(2,1)}), bf16[128,8,768]{2,1,0:T(8,128)(2,1)}, u32[]{:S(2)}, u32[]{:S(2)}) async-start(bf16[128,8,768]{2,1,0:T(8,128)(2,1)} %bitcast.6), calls=%async_computation | async-start | bytes 3145728 | tf_op jit(solution)/shard_map/all_to_all | solution.py:880
  110.3 6.3 %copy-start.19 = (bf16[1024,1536]{1,0:T(8,128)(2,1)S(1)}, bf16[1024,1536]{1,0:T(8,128)(2,1)}, u32[]{:S(2)}) copy-start(bf16[1024,1536]{1,0:T(8,128)(2,1)} %get-tuple-element.52) | copy-start | bytes 9437188
  224.3 4.9 %copy-start.15 = (bf16[384,2304]{1,0:T(8,128)(2,1)S(1)}, bf16[384,2304]{1,0:T(8,128)(2,1)}, u32[]{:S(2)}) copy-start(bf16[384,2304]{1,0:T(8,128)(2,1)} %get-tuple-element.48) | copy-start | bytes 5308420
  229.2 2.0 copy-start.17
  229.2 2.7 %copy-start.16 = (f32[192,768]{1,0:T(8,128)S(1)}, f32[192,768]{1,0:T(8,128)}, u32[]{:S(2)}) copy-start(f32[192,768]{1,0:T(8,128)} %get-tuple-element.67) | copy-start | bytes 1769476
  231.2 1.5 copy-start.18

commit v4 on v3

--- a/solution.py
+++ b/solution.py
@@ -467,7 +467,9 @@
     gqkv_ref,
     gout_w_ref,
     grouter_ref,
-    gsmall_ref,
+    ggain_one_ref,
+    ggain_two_ref,
+    gtable_ref,
     att_all,
     dqkv,
     sums,
@@ -777,9 +779,12 @@
         gout_w_ref[:, block * 128 : (block + 1) * 128] = load(2, block * half, half)
     g_router = sum(load(side, tile_rows, half).astype(F32) for side in range(2))
     grouter_ref[...] = g_router.T[:experts]
-    gsmall_ref[...] = sum(
+    g_small = sum(
         load(side, tile_rows + half, 16 + buckets // 2).astype(F32) for side in range(2)
     )
+    ggain_one_ref[...] = g_small[:blocks]
+    ggain_two_ref[...] = g_small[blocks : 2 * blocks]
+    gtable_ref[...] = g_small[16:, :heads]
 
 
 def back(sizes, dims, sent, result, dispatch, cotangent, tokens, kept, w_out, bucket_row):
@@ -799,7 +804,9 @@
         ((half, 3 * width), BF16),
         ((half, width), BF16),
         ((experts, half), F32),
-        ((16 + buckets // 2, 128), F32),
+        ((half // 128, 128), F32),
+        ((half // 128, 128), F32),
+        ((buckets // 2, heads), F32),
     ]
     return pl.pallas_call(
         functools.partial(back_kernel, sizes, dims, both, cut),
@@ -903,18 +910,18 @@
     grad_back_expert = t_matmul(activated, grad_result)
     grad_in_expert = t_matmul(arrived, grad_pre)
 
-    layer_out, grad_tokens, g_qkv, g_out, g_router, g_small = back(
+    layer_out, grad_tokens, g_qkv, g_out, g_router, g_gain_one, g_gain_two, g_table = back(
         sizes, dims, sent, result, dispatch_two, cotangent, tokens, kept, w_out, bucket_row
     )
 
     return (
         layer_out,
         grad_tokens,
-        g_small[:blocks].reshape(half),
+        g_gain_one.reshape(half),
         g_qkv.astype(F32),
         g_out.astype(F32),
-        g_small[16:, :heads],
-        g_small[blocks : 2 * blocks].reshape(half),
+        g_table,
+        g_gain_two.reshape(half),
         g_router.T,
         grad_in_expert[None],
         grad_back_expert[None],

time: 234 us -> 233 us (level)
    unnamed x45 -> x54, local copies, waits for them, and re-layouts: 11.7 us -> 13.5 us
where the time goes in v4:
time: 233 us
  Pallas kernels  181 us (78%)
  local copies, waits for them, and re-layouts  19.2 us (8%)
  matrix products  10.8 us (5%)
  waiting for transfers between devices  8.94 us (4%)
  other arithmetic  6.57 us (3%)
  starting transfers between devices  5.49 us (2%)
    pallas_call x1, Pallas kernels, back(): pl.pallas_call(functools.partial(back_kernel, sizes, dims, both, cut), ou...  94.4 us
    pallas_call x1, Pallas kernels, front(): pl.pallas_call(functools.partial(front_kernel, sizes, dims), out_shape=[j...  73.5 us
    unnamed x54, local copies, waits for them, and re-layouts  13.5 us
    pallas_call x1, Pallas kernels, expert(): pl.pallas_call(functools.partial(expert_kernel, capacity), grid=(count //...  12.8 us
    dot_general x3, matrix products, dot(): lax.dot_general(a, b, (contract, ((), ())), preferred_element_type=F32)  10.8 us
    all_to_all x1, waiting for transfers between devices, swap_all(): lax.all_to_all(blocks, ('rep', 'shard'), split_axis=0, concat_axis=0, til...  8.94 us
    all_to_all x1, starting transfers between devices, swap_all(): lax.all_to_all(blocks, ('rep', 'shard'), split_axis=0, concat_axis=0, til...  5.49 us
  transfers between devices with their start and end apart: 1, of which 1 were waited for; matrix products, arithmetic and copies ran while one was open for 7% of the time, Pallas kernels for 0%

profile of v4, /device:TPU:1, one launch (start us, length us, event | category | flops | bytes accessed | tf_op | source)
XLA Modules:
  0.0 232.6 jit_solution(15750015084039035621)
XLA Ops:
  1.3 0.9 copy.37
  2.2 0.8 copy.38
  5.2 0.7 fusion.5.small_ref
  5.9 1.1 copy-done.3
  7.0 1.0 copy-done.4
  8.0 1.0 copy-done.5
  8.9 73.5 %shard_map.195 = (bf16[384,768]{1,0:T(8,128)(2,1)S(1)}, bf16[384,1152]{1,0:T(8,128)(2,1)S(1)}, bf16[6,384,384]{2,1,0:T(8,128)(2,1)}, bf16[384,384]{1,0:T(8,128)(...) custom-call(bf16[192,768]{1,0:T(8,128)(2,1)S(1)} %copy-done.4, ...), custom_call_target="tpu_custom_call" | custom-call | flops 30000001024 | bytes 100000000 | tf_op jit(solution)/shard_map/pallas_call | solution.py:350
  82.5 0.9 copy-done.8
  83.4 0.8 copy-done.9
  84.2 1.9 copy-done.7
  86.2 12.8 %shard_map.196 = (bf16[1024,1536]{1,0:T(8,128)(2,1)}, bf16[1024,1536]{1,0:T(8,128)(2,1)}, bf16[1024,768]{1,0:T(8,128)(2,1)}, bf16[1024,768]{1,0:T(8,128)(2,1)S(1)}, bf16[1024,768]{1,0:T(8,128)(2,1)S(1)}) custom-call(bf16[1024,768]{1,0:T(8,128)(2,1)S(1)} %bitcast.23, bf16[1024,768]{1,0:T(8,128)(2,1)S(1)} %bitcast.27, bf16[768,1536]{1,0:T(8,128)(2,1)S(1)} %bitcast.24, ...), custom_call_target="tpu_custom_call" | custom-call | flops 9663676416 | bytes 20000000 | tf_op jit(solution)/shard_map/pallas_call | solution.py:420
  99.0 1.2 copy-done.6
  100.2 5.5 %all-to-all-start = ((bf16[128,8,768]{2,1,0:T(8,128)(2,1)}), bf16[128,8,768]{2,1,0:T(8,128)(2,1)}, u32[]{:S(2)}, u32[]{:S(2)}) async-start(bf16[128,8,768]{2,1,0:T(8,128)(2,1)} %bitcast.6), calls=%async_computation | async-start | bytes 3145728 | tf_op jit(solution)/shard_map/all_to_all | solution.py:887
  105.7 0.8 copy.40
  106.6 1.8 broadcast_in_dim.18
  108.3 2.0 copy.41.dispatch_ref
  110.3 6.3 %convolution_bitcast_fusion.1 = f32[1,768,1536]{2,1,0:T(8,128)} fusion(bf16[1024,1536]{1,0:T(8,128)(2,1)} %get-tuple-element.55, bf16[128,8,768]{2,1,0:T(8,128)(2,1)S(1)} %get-tuple-element.34), kind=kOutput, calls=%fused_computation.1 | convolution fusion | flops 2415919104 | bytes 9437184 | tf_op jit(solution)/shard_map/dot_general | solution.py:75
  116.6 4.3 %convolution_bitcast_fusion = f32[1,1536,768]{2,1,0:T(8,128)} fusion(bf16[1024,1536]{1,0:T(8,128)(2,1)S(1)} %copy-done.22, bf16[1024,768]{1,0:T(8,128)(2,1)S(1)} %get-tuple-element.57), kind=kOutput, calls=%fused_computation | convolution fusion | flops 2415919104 | bytes 9437184 | tf_op jit(solution)/shard_map/dot_general | solution.py:75
  120.9 8.9 %all-to-all-done = bf16[128,8,768]{2,1,0:T(8,128)(2,1)} async-done(((bf16[128,8,768]{2,1,0:T(8,128)(2,1)}), bf16[128,8,768]{2,1,0:T(8,128)(2,1)}, u32[]{:S(2)}, u32[]{:S(2)}) %all-to-all-start) | async-done | bytes 1572896 | tf_op jit(solution)/shard_map/all_to_all | solution.py:887
  129.9 94.4 %shard_map.197 = (bf16[192,768]{1,0:T(8,128)(2,1)}, f32[192,768]{1,0:T(8,128)}, bf16[384,2304]{1,0:T(8,128)(2,1)}, bf16[384,768]{1,0:T(8,128)(2,1)}, f32[64,384]...) custom-call(bf16[1024,768]{1,0:T(8,128)(2,1)} %bitcast.7.sent_ref, ...), custom_call_target="tpu_custom_call" | custom-call | flops 60000002048 | bytes 200000000 | tf_op jit(solution)/shard_map/pallas_call | solution.py:811
  224.3 2.3 convert_element_type.38
  226.6 2.0 convert_element_type.37
  228.7 0.7 copy.48
  229.4 0.8 copy.49
  (52 shorter events, 5.3 us)
Async XLA Ops:
  1.3 81.1 %copy-start = (s32[1,384]{1,0:T(1,128)}, s32[1,384]{1,0:T(1,128)S(1)}, u32[]{:S(2)}) copy-start(s32[1,384]{1,0:T(1,128)S(1)} %reshape.67.bucket_ref) | copy-start | bytes 4612
  5.9 1.1 copy-start.3
  7.0 1.0 copy-start.4
  7.9 1.0 copy-start.5
  8.9 75.3 %copy-start.1 = (bf16[1,768,1536]{2,1,0:T(8,128)(2,1)S(1)}, bf16[1,768,1536]{2,1,0:T(8,128)(2,1)}, u32[]{:S(2)}) copy-start(bf16[1,768,1536]{2,1,0:T(8,128)(2,1)} %param.21) | copy-start | bytes 7077892
  8.9 75.3 %copy-start.2 = (bf16[1,1536,768]{2,1,0:T(8,128)(2,1)S(1)}, bf16[1,1536,768]{2,1,0:T(8,128)(2,1)}, u32[]{:S(2)}) copy-start(bf16[1,1536,768]{2,1,0:T(8,128)(2,1)} %param.22) | copy-start | bytes 7077892
  82.5 0.9 copy-start.8
  83.4 0.8 copy-start.9
  84.2 14.7 %copy-start.10 = (f32[192,768]{1,0:T(8,128)}, f32[192,768]{1,0:T(8,128)S(1)}, u32[]{:S(2)}) copy-start(f32[192,768]{1,0:T(8,128)S(1)} %get-tuple-element.44.hidden_ref) | copy-start | bytes 1769476
  84.2 14.7 %copy-start.11 = (bf16[384,384]{1,0:T(8,128)(2,1)}, bf16[384,384]{1,0:T(8,128)(2,1)S(1)}, u32[]{:S(2)}) copy-start(bf16[384,384]{1,0:T(8,128)(2,1)S(1)} %get-tuple-element.41.mixed_ref) | copy-start | bytes 884740
  84.2 14.7 %copy-start.12 = (bf16[192,768]{1,0:T(8,128)(2,1)}, bf16[192,768]{1,0:T(8,128)(2,1)S(1)}, u32[]{:S(2)}) copy-start(bf16[192,768]{1,0:T(8,128)(2,1)S(1)} %get-tuple-element.45.n2_ref) | copy-start | bytes 884740
  84.2 14.7 %copy-start.13 = (bf16[2,416,128]{2,1,0:T(8,128)(2,1)}, bf16[2,416,128]{2,1,0:T(8,128)(2,1)S(1)}, u32[]{:S(2)}) copy-start(bf16[2,416,128]{2,1,0:T(8,128)(2,1)S(1)} %get-tuple-element.43.small_all) | copy-start | bytes 638980
  84.2 14.8 %copy-start.14 = (f32[192,128]{1,0:T(8,128)}, f32[192,128]{1,0:T(8,128)S(1)}, u32[]{:S(2)}) copy-start(f32[192,128]{1,0:T(8,128)S(1)} %get-tuple-element.46.router_ref) | copy-start | bytes 294916
  84.2 1.9 copy-start.7
  99.0 1.2 copy-start.6
  100.2 29.7 %all-to-all-start = ((bf16[128,8,768]{2,1,0:T(8,128)(2,1)}), bf16[128,8,768]{2,1,0:T(8,128)(2,1)}, u32[]{:S(2)}, u32[]{:S(2)}) async-start(bf16[128,8,768]{2,1,0:T(8,128)(2,1)} %bitcast.6), calls=%async_computation | async-start | bytes 3145728 | tf_op jit(solution)/shard_map/all_to_all | solution.py:887
  110.3 6.3 %copy-start.22 = (bf16[1024,1536]{1,0:T(8,128)(2,1)S(1)}, bf16[1024,1536]{1,0:T(8,128)(2,1)}, u32[]{:S(2)}) copy-start(bf16[1024,1536]{1,0:T(8,128)(2,1)} %get-tuple-element.56) | copy-start | bytes 9437188
  224.3 2.3 copy-start.15
  226.6 2.0 copy-start.17
  226.6 2.8 %copy-start.16 = (f32[192,768]{1,0:T(8,128)S(1)}, f32[192,768]{1,0:T(8,128)}, u32[]{:S(2)}) copy-start(f32[192,768]{1,0:T(8,128)} %get-tuple-element.69) | copy-start | bytes 1769476
  228.7 1.6 copy-start.21
  228.7 2.1 copy-start.19
  228.7 2.7 %copy-start.20 = (f32[3,128]{1,0:T(4,128)S(1)}, f32[3,128]{1,0:T(4,128)}, u32[]{:S(2)}) copy-start(f32[3,128]{1,0:T(4,128)} %get-tuple-element.53) | copy-start | bytes 4612
  228.7 3.3 %copy-start.18 = (f32[64,384]{1,0:T(8,128)S(1)}, f32[64,384]{1,0:T(8,128)}, u32[]{:S(2)}) copy-start(f32[64,384]{1,0:T(8,128)} %get-tuple-element.54) | copy-start | bytes 294916
